TPU v7x, 512 devices: a whole 4x8x8 slice. The times are simulated.
512 devices in a mesh: lead: 32 (over z_lo, y, core), tile: 16 (over x, z_hi).
Axes of the slice: x: 4, y: 8, z: 8 (z_hi: 4, z_lo: 2; z = z_hi * 2 + z_lo), core: 2. Of those that a mesh axis runs over, the one named last changes fastest.
Arguments:
- frames: bfloat16 [3, 384, 16, 128], P(None, None, 'tile'), may hold values from -6 to 6
- enc_weight: bfloat16 [384, 4, 9, 768], P('lead'), may hold values from -0.078125 to 0.078125
- enc_bias: float32 [384, 4], P('lead'), may hold values from -4 to 4
- head_weight: bfloat16 [384, 9, 384], replicated, may hold values from -0.109375 to 0.109375
- film_table: float32 [16, 2, 384], replicated, may hold values from -2.5 to 2.5
- lead_index: int32 [32], P('lead'), may hold values from 0 to 15
- cotangent: bfloat16 [32, 384, 16, 128], P('lead', None, 'tile'), may hold values from -6 to 6
Outputs:
- enc_weight_grad: bfloat16 [384, 4, 9, 768], P('lead')
- enc_bias_grad: float32 [384, 4], P('lead')
- head_weight_grad: bfloat16 [384, 9, 384], P('tile')
- film_grad: float32 [16, 2, 384], replicated
All inputs are finite; a program needn't handle non-finite values.
Results may differ from a plain program's by a relative error of at most 0.0052.
Values may be sent and summed in bfloat16 or wider, within the bound.
A program may use at most 128 MiB of HBM per device.

v0:
```python
import math

import jax
import jax.numpy as jnp
from jax import lax
from jax.sharding import PartitionSpec as P

tap_offsets = [(row_off, col_off) for row_off in (-1, 0, 1) for col_off in (-1, 0, 1)]


def extended(x, sides, width):
    for axis, dim in sides:
        size, length = (lax.axis_size(axis), x.shape[dim])
        up = [(i, (i + 1) % size) for i in range(size - 1)]
        down = [(j, i) for i, j in up]
        last = lax.slice_in_dim(x, length - width, length, axis=dim)
        leading = lax.slice_in_dim(x, 0, width, axis=dim)
        before = lax.ppermute(last, axis, up)
        after = lax.ppermute(leading, axis, down)
        x = jnp.concatenate([before, x, after], axis=dim)
    return x


def from_behind(x, axis, by):
    length = lax.axis_size(axis)
    pairs = [(i, i + by) for i in range(length) if 0 <= i + by < length]
    return lax.ppermute(x, axis, pairs)


def shift_cols(field_in, offset):
    col_count = field_in.shape[-1]
    if offset == 0:
        return field_in
    lead_pads = [(0, 0)] * (field_in.ndim - 1)
    if offset > 0:
        return jnp.pad(field_in[..., offset:], lead_pads + [(0, offset)])
    return jnp.pad(field_in[..., : col_count + offset], lead_pads + [(-offset, 0)])


def near_rows(field_in):
    return extended(field_in, (("tile", 1),), 1)


def far_rows(field_in, by_tiles):
    return from_behind(field_in, "tile", by_tiles)


def padded_taps(padded, row_count, direction):
    pieces = []
    for row_off, col_off in tap_offsets:
        first_row = 1 + direction * row_off
        pieces.append(
            shift_cols(padded[:, first_row : first_row + row_count, :], direction * col_off)
        )
    return jnp.stack(pieces, 0)


def lead_total(partial_sum):
    owned_sum = lax.psum_scatter(partial_sum, "lead", scatter_dimension=0, tiled=True)
    return owned_sum


def shards(frames, enc_weight, enc_bias, head_weight, film_table, lead_index, cotangent):
    owned, gate_count, tap_count, channels = enc_weight.shape
    in_chan = frames.shape[1]
    row_count = frames.shape[2]
    col_count = frames.shape[3]
    hidden = head_weight.shape[0]
    dilation = 2 * row_count
    lead_count = lax.axis_size("lead")
    tile_count = lax.axis_size("tile")
    loss_scale = 1.0 / math.sqrt(lead_count * row_count * tile_count * col_count)
    h_full = jnp.zeros((hidden, row_count, col_count), jnp.bfloat16)
    cell_memory = jnp.zeros((owned, row_count, col_count), jnp.float32)
    saved = []
    for step_index in range(frames.shape[0]):
        stacked = jnp.concatenate([frames[step_index], h_full], 0)
        fwd_taps = padded_taps(near_rows(stacked), row_count, 1)
        preact = jnp.einsum(
            "ojkc,kcrw->ojrw", enc_weight, fwd_taps, preferred_element_type=jnp.float32
        )
        preact = preact + enc_bias[:, :, None, None]
        in_gate = jax.nn.sigmoid(preact[:, 0])
        forget = jax.nn.sigmoid(preact[:, 1])
        cand_gate = jnp.tanh(preact[:, 2])
        output_gate = jax.nn.sigmoid(preact[:, 3])
        previous = cell_memory
        cell_memory = forget * previous + in_gate * cand_gate
        h_owned = (output_gate * jnp.tanh(cell_memory)).astype(jnp.bfloat16)
        h_full = lax.all_gather(h_owned, "lead", axis=0, tiled=True)
        saved.append((fwd_taps, in_gate, forget, cand_gate, output_gate, previous, cell_memory))
    chosen = (jnp.arange(film_table.shape[0]) == lead_index[0]).astype(jnp.float32)
    film_rows = jnp.sum(chosen[:, None, None] * film_table, 0)
    film_scale = 1.0 + film_rows[0]
    film_shift = film_rows[1]
    enc_wide = h_full.astype(jnp.float32)
    modulated = film_scale[:, None, None] * enc_wide + film_shift[:, None, None]
    activated_output = jax.nn.silu(modulated).astype(jnp.bfloat16)
    cotangent_lead = cotangent[0]
    pair_stack = jnp.stack([activated_output, cotangent_lead], 0)
    from_above = far_rows(pair_stack, 2)
    from_below = far_rows(pair_stack, -2)
    act_rows = {-1: from_above[0], 0: activated_output, 1: from_below[0]}
    cot_rows = {-1: from_below[1], 0: cotangent_lead, 1: from_above[1]}
    activation_taps = jnp.stack(
        [shift_cols(act_rows[row_off], dilation * col_off) for row_off, col_off in tap_offsets], 0
    )
    cotangent_taps = jnp.stack(
        [shift_cols(cot_rows[row_off], -dilation * col_off) for row_off, col_off in tap_offsets], 0
    )
    act_grad = jnp.einsum(
        "okc,korw->crw", head_weight, cotangent_taps, preferred_element_type=jnp.float32
    )
    logistic = jax.nn.sigmoid(modulated)
    mod_grad = act_grad * logistic * (1.0 + modulated * (1.0 - logistic))
    film_stats = jnp.stack(
        [jnp.sum(mod_grad * enc_wide, axis=(1, 2)), jnp.sum(mod_grad, axis=(1, 2))], 0
    )
    hid_grad = cotangent_lead.astype(jnp.float32) + film_scale[:, None, None] * mod_grad
    block_rows = hidden // tile_count
    full_term = jnp.einsum(
        "orw,kcrw->okc", cotangent_lead, activation_taps, preferred_element_type=jnp.float32
    )
    blocks = full_term.reshape(tile_count, block_rows, tap_count, hidden)
    received = lax.all_to_all(blocks, "tile", split_axis=0, concat_axis=0, tiled=True)
    head_shard = jnp.sum(received, 0)
    hid_owned = lead_total(hid_grad)
    mem_grad = jnp.zeros((owned, row_count, col_count), jnp.float32)
    weight_grad = jnp.zeros((owned, gate_count, tap_count, channels), jnp.float32)
    bias_grad = jnp.zeros((owned, gate_count), jnp.float32)
    flat_weight = enc_weight.reshape(owned * gate_count, tap_count, channels)[:, :, in_chan:]
    for step_index in reversed(range(frames.shape[0])):
        fwd_taps, in_gate, forget, cand_gate, output_gate, previous, cell_memory = saved[step_index]
        squashed = jnp.tanh(cell_memory)
        mem_grad = mem_grad + hid_owned * output_gate * (1.0 - squashed * squashed)
        gate_grad = jnp.stack(
            [
                mem_grad * cand_gate * in_gate * (1.0 - in_gate),
                mem_grad * previous * forget * (1.0 - forget),
                mem_grad * in_gate * (1.0 - cand_gate * cand_gate),
                hid_owned * squashed * output_gate * (1.0 - output_gate),
            ],
            1,
        )
        gate_low = gate_grad.astype(jnp.bfloat16)
        weight_grad = weight_grad + jnp.einsum(
            "ojrw,kcrw->ojkc", gate_low, fwd_taps, preferred_element_type=jnp.float32
        )
        bias_grad = bias_grad + jnp.sum(gate_grad, axis=(2, 3))
        if step_index > 0:
            flat_grad = gate_low.reshape(owned * gate_count, row_count, col_count)
            back_taps = padded_taps(near_rows(flat_grad), row_count, -1)
            partial_sum = jnp.einsum(
                "okc,korw->crw", flat_weight, back_taps, preferred_element_type=jnp.float32
            )
            hid_owned = lead_total(partial_sum)
            mem_grad = mem_grad * forget
    weight_sum, bias_sum, stats_sum = lax.psum((weight_grad, bias_grad, film_stats), "tile")
    dense_table = chosen[:, None, None] * stats_sum[None]
    head_total, table_total = lax.psum((head_shard, dense_table), "lead")
    head_out = (head_total * loss_scale).astype(jnp.bfloat16)
    return (
        (weight_sum * loss_scale).astype(jnp.bfloat16),
        bias_sum * loss_scale,
        head_out,
        table_total * loss_scale,
    )


def solution(mesh):
    in_specs = (
        P(None, None, "tile", None),
        P("lead", None, None, None),
        P("lead", None),
        P(),
        P(),
        P("lead"),
        P("lead", None, "tile", None),
    )
    out_specs = (P("lead", None, None, None), P("lead", None), P("tile", None, None), P())
    return jax.shard_map(shards, mesh=mesh, in_specs=in_specs, out_specs=out_specs, check_vma=False)
```

profile of v0, /device:TPU:1, one launch (start us, length us, event | category | flops | bytes accessed | tf_op | source)
XLA Modules:
  0.0 1099.8 jit_solution(7019664390748805517)
XLA Ops:
  7.2 1.2 slice_bitcast_fusion.2
  9.0 1.3 collective-permute-start.1
  10.3 7.3 collective-permute-start
  19.0 1.0 copy.244
  21.1 1.3 collective-permute-done.1
  24.9 40.9 %all_gather.9 = bf16[384,1,128]{2,1,0:T(2,128)(2,1)S(1)} all-gather(bf16[12,1,128]{2,1,0:T(2,128)(2,1)S(1)} %get-tuple-element.69), channel_id=1, replica_groups=mesh['lead'=32,'tile'=16] {'lead'}, dimensions={0}, use_global_device_ids=true | all-gather | bytes 101376 | tf_op jit(solution)/shard_map/all_gather | solution.py:90
  65.8 5.0 collective-permute-start.2
  70.9 1.3 collective-permute-start.3
  72.3 2.6 collective-permute-done.2
  75.6 13.1 %collective-permute-done.3 = bf16[768,1,128]{2,0,1:T(8,128)(2,1)S(1)} collective-permute-done((bf16[768,1,128]{2,0,1:T(8,128)(2,1)S(1)}, bf16[768,1,128]{2,0,1:T(8,128)(2,1)S(1)}, u32[]{:S(2)}, u32[]{:S(2)}) %collective-permute-start.3) | collective-permute-done | bytes 196640 | tf_op jit(solution)/shard_map/ppermute | solution.py:19
  91.0 31.2 %all_gather.10 = bf16[384,1,128]{2,1,0:T(2,128)(2,1)S(1)} all-gather(bf16[12,1,128]{2,1,0:T(2,128)(2,1)S(1)} %get-tuple-element.64), channel_id=1, replica_groups=mesh['lead'=32,'tile'=16] {'lead'}, dimensions={0}, use_global_device_ids=true | all-gather | bytes 101376 | tf_op jit(solution)/shard_map/all_gather | solution.py:90
  122.2 5.5 collective-permute-start.4
  127.7 1.3 collective-permute-start.5
  129.2 2.7 collective-permute-done.4
  132.5 9.8 collective-permute-done.5
  144.7 31.2 %all_gather.11 = bf16[384,1,128]{2,1,0:T(2,128)(2,1)S(1)} all-gather(bf16[12,1,128]{2,1,0:T(2,128)(2,1)S(1)} %get-tuple-element.59), channel_id=1, replica_groups=mesh['lead'=32,'tile'=16] {'lead'}, dimensions={0}, use_global_device_ids=true | all-gather | bytes 101376 | tf_op jit(solution)/shard_map/all_gather | solution.py:90
  176.2 11.2 %collective-permute-start.7 = (bf16[2,384,1,128]{1,3,2,0:T(8,128)(2,1)S(1)}, bf16[2,384,1,128]{1,3,2,0:T(8,128)(2,1)S(1)}, u32[]{:S(2)}, u32[]{:S(2)}) collective-permute-start(bf16[2,384,1,128]{1,3,2,0:T(8,128)(2,1)S(1)} %pad_maximum_fusion.2), channel_id=1, source_target_pairs={{0,2},{1,3},{2,4},{3,5},{4,6},{5,7},{6,8},{7,9},{8,10},{9,11},{10,... | collective-permute-start | bytes 589832 | tf_op jit(solution)/shard_map/ppermute | solution.py:27
  187.4 1.3 collective-permute-start.6
  188.8 4.0 collective-permute-done.7
  192.8 9.7 collective-permute-done.6
  203.8 2.7 copy.316
  206.5 9.3 all-to-all-start
  216.8 0.9 constant_dynamic-update-slice_fusion.4
  217.9 2.0 fusion.39
  220.8 2.2 copy.305
  222.9 1.5 reshape.988
  224.5 1.3 dynamic-slice
  226.4 210.0 %all-reduce.55.cloned.1.call-done = f32[384,1,128]{2,1,0:T(1,128)} async-done(((f32[384,1,128]{2,1,0:T(1,128)}), f32[384,1,128]{2,1,0:T(1,128)}) %all-reduce.55.cloned.1.call-update) | async-done | bytes 196624
  436.4 1.3 fusion.102
  438.4 3.7 collective-permute-start.9
  442.1 1.3 collective-permute-start.8
  443.5 4.9 collective-permute-done.8
  450.1 1.4 maximum_bitcast_fusion
  451.4 210.9 %all-reduce.57.cloned.1.call-done = f32[384,1,128]{2,1,0:T(1,128)} async-done(((f32[384,1,128]{2,1,0:T(1,128)}), f32[384,1,128]{2,1,0:T(1,128)}) %all-reduce.57.cloned.1.call-update) | async-done | bytes 196624
  662.3 1.4 fusion.98
  663.7 1.3 fusion.99
  665.1 3.7 collective-permute-start.11
  668.8 1.5 collective-permute-start.10
  670.4 4.7 collective-permute-done.10
  676.7 3.5 reduce_sum.67
  680.4 3.6 fusion
  684.1 2.0 fusion.4
  686.0 206.7 %all-reduce.59.cloned.1.call-done = (f32[384,1,128]{2,1,0:T(1,128)}, f32[24,9,384]{2,0,1:T(8,128)}) async-done(((f32[384,1,128]{2,1,0:T(1,128)}, f32[24,9,384]{2,0,1:T(8,128)}), (f32[384,1,128]{2,1,0:T(1,128)}, f32[24,9,384]{2,0,1:T(8,128)})) %all-reduce.59.cloned.1.call-update) | async-done | bytes 528400
  893.6 4.5 add_add_fusion
  899.3 71.0 %all-reduce.47 = (f32[12,4]{1,0:T(8,128)S(1)}, f32[2,384]{1,0:T(2,128)S(1)}) all-reduce(f32[12,4]{1,0:T(8,128)S(1)} %add_add_fusion.1, f32[2,384]{1,0:T(2,128)S(1)} %pad_maximum_fusion.5), channel_id=1, replica_groups=mesh['lead'=32,'tile'=16] {'tile'}, use_global_device_ids=true, to_apply=%region_8.9 | all-reduce | flops 816 | bytes 6528 | tf_op jit(solution)/shard_map/psum | solution.py:158
  971.0 118.1 %psum.39 = f32[16,2,384]{2,1,0:T(2,128)S(1)} all-reduce(f32[16,2,384]{2,1,0:T(2,128)S(1)} %broadcast_multiply_fusion.1), channel_id=1, replica_groups=mesh['lead'=32,'tile'=16] {'lead'}, use_global_device_ids=true, to_apply=%region_14.15 | all-reduce | flops 12288 | bytes 98304 | tf_op jit(solution)/shard_map/psum | solution.py:160
  1090.5 1.6 multiply_convert_fusion
  1092.1 1.2 copy.317
  (252 shorter events, 22.7 us)
Async XLA Ops:
  7.2 210.7 %copy-start = (bf16[384,9,384]{2,0,1:T(8,128)(2,1)S(1)}, bf16[384,9,384]{2,0,1:T(8,128)(2,1)}, u32[]{:S(2)}) copy-start(bf16[384,9,384]{2,0,1:T(8,128)(2,1)} %param.10) | copy-start | bytes 7962628
  9.0 13.4 %collective-permute-start.1 = (bf16[768,1,128]{2,0,1:T(8,128)(2,1)}, bf16[768,1,128]{2,0,1:T(8,128)(2,1)S(1)}, u32[]{:S(2)}, u32[]{:S(2)}) collective-permute-start(bf16[768,1,128]{2,0,1:T(8,128)(2,1)} %concatenate.21), channel_id=1, source_target_pairs={{1,0},{2,1},{3,2},{4,3},{5,4},{6,5},{7,6},{8,7},{9,8},{10,9},{11,1... | collective-permute-start | bytes 589832 | tf_op jit(solution)/shard_map/ppermute | solution.py:19
  10.3 10.2 collective-permute-start
  20.1 50.7 %copy-start.49 = (f32[16]{0:T(128)}, f32[16]{0:T(128)S(1)}, u32[]{:S(2)}) copy-start(f32[16]{0:T(128)S(1)} %compare_convert_fusion) | copy-start | bytes 196
  22.8 48.0 %copy-start.36 = (f32[16,2,384]{2,1,0:T(2,128)S(1)}, f32[16,2,384]{2,1,0:T(2,128)}, u32[]{:S(2)}) copy-start(f32[16,2,384]{2,1,0:T(2,128)} %param.11) | copy-start | bytes 147460
  24.2 51.1 %copy-start.12 = (f32[12,4,1,128]{3,1,0,2:T(4,128)}, f32[12,4,1,128]{3,1,0,2:T(4,128)S(1)}, u32[]{:S(2)}) copy-start(f32[12,4,1,128]{3,1,0,2:T(4,128)S(1)} %get-tuple-element.119) | copy-start | bytes 73732
  65.8 9.1 collective-permute-start.2
  70.9 17.7 %collective-permute-start.3 = (bf16[768,1,128]{2,0,1:T(8,128)(2,1)S(1)}, bf16[768,1,128]{2,0,1:T(8,128)(2,1)S(1)}, u32[]{:S(2)}, u32[]{:S(2)}) collective-permute-start(bf16[768,1,128]{2,0,1:T(8,128)(2,1)S(1)} %pad_maximum_fusion), channel_id=1, source_target_pairs={{1,0},{2,1},{3,2},{4,3},{5,4},{6,5},{7,6},{8,7},{9,8},{10,9},{11,1... | collective-permute-start | bytes 589832 | tf_op jit(solution)/shard_map/ppermute | solution.py:19
  122.2 9.6 collective-permute-start.4
  127.7 48.4 %copy-start.37 = (f32[384]{0:T(512)}, f32[384]{0:T(512)S(1)}, u32[]{:S(2)}) copy-start(f32[384]{0:T(512)S(1)} %get-tuple-element.26) | copy-start | bytes 4612
  127.7 48.4 %copy-start.39 = (f32[384]{0:T(512)}, f32[384]{0:T(512)S(1)}, u32[]{:S(2)}) copy-start(f32[384]{0:T(512)S(1)} %get-tuple-element.27) | copy-start | bytes 4612
  127.7 14.6 %collective-permute-start.5 = (bf16[768,1,128]{2,0,1:T(8,128)(2,1)S(1)}, bf16[768,1,128]{2,0,1:T(8,128)(2,1)S(1)}, u32[]{:S(2)}, u32[]{:S(2)}) collective-permute-start(bf16[768,1,128]{2,0,1:T(8,128)(2,1)S(1)} %pad_maximum_fusion.1), channel_id=1, source_target_pairs={{1,0},{2,1},{3,2},{4,3},{5,4},{6,5},{7,6},{8,7},{9,8},{10,9},{11,1... | collective-permute-start | bytes 589832 | tf_op jit(solution)/shard_map/ppermute | solution.py:19
  176.2 26.5 %copy-start.38 = (f32[384]{0:T(512)S(1)}, f32[384]{0:T(512)}, u32[]{:S(2)}) copy-start(f32[384]{0:T(512)} %copy-done.37) | copy-start | bytes 4612
  176.2 26.5 %copy-start.40 = (f32[384]{0:T(512)S(1)}, f32[384]{0:T(512)}, u32[]{:S(2)}) copy-start(f32[384]{0:T(512)} %copy-done.39) | copy-start | bytes 4612
  176.2 16.5 %collective-permute-start.7 = (bf16[2,384,1,128]{1,3,2,0:T(8,128)(2,1)S(1)}, bf16[2,384,1,128]{1,3,2,0:T(8,128)(2,1)S(1)}, u32[]{:S(2)}, u32[]{:S(2)}) collective-permute-start(bf16[2,384,1,128]{1,3,2,0:T(8,128)(2,1)S(1)} %pad_maximum_fusion.2), channel_id=1, source_target_pairs={{0,2},{1,3},{2,4},{3,5},{4,6},{5,7},{6,8},{7,9},{8,10},{9,11},{10,... | collective-permute-start | bytes 589832 | tf_op jit(solution)/shard_map/ppermute | solution.py:27
  187.4 15.1 %collective-permute-start.6 = (bf16[2,384,1,128]{1,3,2,0:T(8,128)(2,1)S(1)}, bf16[2,384,1,128]{1,3,2,0:T(8,128)(2,1)S(1)}, u32[]{:S(2)}, u32[]{:S(2)}) collective-permute-start(bf16[2,384,1,128]{1,3,2,0:T(8,128)(2,1)S(1)} %pad_maximum_fusion.2), channel_id=1, source_target_pairs={{2,0},{3,1},{4,2},{5,3},{6,4},{7,5},{8,6},{9,7},{10,8},{11,9},{12,... | collective-permute-start | bytes 589832 | tf_op jit(solution)/shard_map/ppermute | solution.py:27
  188.8 14.2 %copy-start.5 = (bf16[1,384,1,128]{3,1,2,0:T(8,128)(2,1)S(1)}, bf16[1,384,1,128]{3,1,2,0:T(8,128)(2,1)}, u32[]{:S(2)}) copy-start(bf16[1,384,1,128]{3,1,2,0:T(8,128)(2,1)} %param.13) | copy-start | bytes 294916
  206.5 470.2 %all-to-all-start = ((f32[16,24,9,384]{3,1,2,0:T(8,128)}), f32[16,24,9,384]{3,1,2,0:T(8,128)}, u32[]{:S(2)}, u32[]{:S(2)}) async-start(f32[16,24,9,384]{3,1,2,0:T(8,128)} %copy.316), calls=%async_computation | async-start | bytes 10616832 | tf_op jit(solution)/shard_map/all_to_all | solution.py:125
  215.8 220.5 %all-reduce.55.cloned.1.call-start = ((), (), s32[]{:S(2)}) async-start(), calls=%async_computation.2 | async-start | bytes 393216
  219.9 216.5 %copy-start.11 = (f32[12,4,1,128]{3,1,2,0:T(4,128)S(1)}, f32[12,4,1,128]{3,1,2,0:T(4,128)}, u32[]{:S(2)}) copy-start(f32[12,4,1,128]{3,1,2,0:T(4,128)} %copy-done.10) | copy-start | bytes 73732
  219.9 216.5 %copy-start.35 = (f32[12,1,128]{2,1,0:T(1,128)S(1)}, f32[12,1,128]{2,1,0:T(1,128)}, u32[]{:S(2)}) copy-start(f32[12,1,128]{2,1,0:T(1,128)} %get-tuple-element.62) | copy-start | bytes 18436
  219.9 216.5 %copy-start.47 = (f32[12,1,128]{2,1,0:T(1,128)S(1)}, f32[12,1,128]{2,1,0:T(1,128)}, u32[]{:S(2)}) copy-start(f32[12,1,128]{2,1,0:T(1,128)} %get-tuple-element.60) | copy-start | bytes 18436
  219.9 216.5 %copy-start.48 = (f32[12,1,128]{2,1,0:T(1,128)S(1)}, f32[12,1,128]{2,1,0:T(1,128)}, u32[]{:S(2)}) copy-start(f32[12,1,128]{2,1,0:T(1,128)} %get-tuple-element.63) | copy-start | bytes 18436
  219.9 217.8 %copy-start.29 = (f32[12,1,128]{2,1,0:T(1,128)S(1)}, f32[12,1,128]{2,1,0:T(1,128)}, u32[]{:S(2)}) copy-start(f32[12,1,128]{2,1,0:T(1,128)} %get-tuple-element.61) | copy-start | bytes 18436
  220.7 441.6 %all-reduce.57.cloned.1.call-start = ((), (), s32[]{:S(2)}) async-start(), calls=%async_computation.3 | async-start | bytes 393216
  222.9 439.4 %copy-start.9 = (f32[12,4,1,128]{3,1,0,2:T(4,128)S(1)}, f32[12,4,1,128]{3,1,0,2:T(4,128)}, u32[]{:S(2)}) copy-start(f32[12,4,1,128]{3,1,0,2:T(4,128)} %copy-done.8) | copy-start | bytes 73732
  437.7 11.1 %copy-start.30 = (f32[12,1,128]{2,1,0:T(1,128)}, f32[12,1,128]{2,1,0:T(1,128)S(1)}, u32[]{:S(2)}) copy-start(f32[12,1,128]{2,1,0:T(1,128)S(1)} %get-tuple-element.51) | copy-start | bytes 18436
  437.7 11.1 %copy-start.32 = (f32[12,1,128]{2,1,0:T(1,128)}, f32[12,1,128]{2,1,0:T(1,128)S(1)}, u32[]{:S(2)}) copy-start(f32[12,1,128]{2,1,0:T(1,128)S(1)} %get-tuple-element.82) | copy-start | bytes 18436
  437.7 11.1 %copy-start.34 = (f32[12,1,128]{2,1,0:T(1,128)}, f32[12,1,128]{2,1,0:T(1,128)S(1)}, u32[]{:S(2)}) copy-start(f32[12,1,128]{2,1,0:T(1,128)S(1)} %get-tuple-element.52) | copy-start | bytes 18436
  438.3 10.5 copy-start.16
  438.3 10.5 copy-start.18
  438.4 10.3 collective-permute-start.9
  442.1 6.3 collective-permute-start.8
  450.0 442.8 %all-reduce.59.cloned.1.call-start = ((), (), s32[]{:S(2)}) async-start(), calls=%async_computation.4 | async-start | bytes 1056768
  663.7 11.8 %copy-start.20 = (f32[12,1,128]{2,1,0:T(1,128)}, f32[12,1,128]{2,1,0:T(1,128)S(1)}, u32[]{:S(2)}) copy-start(f32[12,1,128]{2,1,0:T(1,128)S(1)} %get-tuple-element.42) | copy-start | bytes 18436
  663.7 11.8 %copy-start.22 = (f32[12,1,128]{2,1,0:T(1,128)}, f32[12,1,128]{2,1,0:T(1,128)S(1)}, u32[]{:S(2)}) copy-start(f32[12,1,128]{2,1,0:T(1,128)S(1)} %get-tuple-element.80) | copy-start | bytes 18436
  663.7 11.8 %copy-start.26 = (f32[12,1,128]{2,1,0:T(1,128)}, f32[12,1,128]{2,1,0:T(1,128)S(1)}, u32[]{:S(2)}) copy-start(f32[12,1,128]{2,1,0:T(1,128)S(1)} %get-tuple-element.43) | copy-start | bytes 18436
  665.1 10.3 collective-permute-start.11
  668.8 6.3 collective-permute-start.10
  680.3 410.2 %all-reduce.53.cloned.1.call-start = ((), (), s32[]{:S(2)}) async-start(), calls=%async_computation.1 | async-start | bytes 3538944 | tf_op jit(solution)/shard_map/psum | solution.py:158
  684.0 208.8 %copy-start.13 = (f32[12,4,1,128]{3,1,0,2:T(4,128)S(1)}, f32[12,4,1,128]{3,1,0,2:T(4,128)}, u32[]{:S(2)}) copy-start(f32[12,4,1,128]{3,1,0,2:T(4,128)} %copy-done.12) | copy-start | bytes 73732
  684.0 208.7 %copy-start.15 = (f32[12,1,128]{2,1,0:T(1,128)S(1)}, f32[12,1,128]{2,1,0:T(1,128)}, u32[]{:S(2)}) copy-start(f32[12,1,128]{2,1,0:T(1,128)} %get-tuple-element.72) | copy-start | bytes 18436
  684.0 208.7 %copy-start.27 = (f32[12,1,128]{2,1,0:T(1,128)S(1)}, f32[12,1,128]{2,1,0:T(1,128)}, u32[]{:S(2)}) copy-start(f32[12,1,128]{2,1,0:T(1,128)} %copy-done.26) | copy-start | bytes 18436
  684.0 208.7 %copy-start.28 = (f32[12,1,128]{2,1,0:T(1,128)S(1)}, f32[12,1,128]{2,1,0:T(1,128)}, u32[]{:S(2)}) copy-start(f32[12,1,128]{2,1,0:T(1,128)} %get-tuple-element.66) | copy-start | bytes 18436
  684.0 208.7 %copy-start.42 = (f32[12,1,128]{2,1,0:T(1,128)S(1)}, f32[12,1,128]{2,1,0:T(1,128)}, u32[]{:S(2)}) copy-start(f32[12,1,128]{2,1,0:T(1,128)} %get-tuple-element.73) | copy-start | bytes 18436
  684.1 209.5 %copy-start.41 = (f32[12,1,128]{2,1,0:T(1,128)S(1)}, f32[12,1,128]{2,1,0:T(1,128)}, u32[]{:S(2)}) copy-start(f32[12,1,128]{2,1,0:T(1,128)} %get-tuple-element.71) | copy-start | bytes 18436
  898.2 72.7 %copy-start.50 = (f32[16]{0:T(128)S(1)}, f32[16]{0:T(128)}, u32[]{:S(2)}) copy-start(f32[16]{0:T(128)} %copy-done.49) | copy-start | bytes 196
  898.2 191.6 %copy-start.7 = (f32[24,9,384]{2,0,1:T(8,128)S(1)}, f32[24,9,384]{2,0,1:T(8,128)}, u32[]{:S(2)}) copy-start(f32[24,9,384]{2,0,1:T(8,128)} %get-tuple-element.29) | copy-start | bytes 995332
  (22 other events, 46.3 us)
Sparse Core Ops, SparseCore 0:
  220.8 215.4 all-reduce.54
  450.1 212.1 all-reduce.56
  680.4 212.3 all-reduce.58
  898.4 173.1 all-reduce.52
where the time goes:
time: 1100 us
  waiting for transfers between devices  681 us (62%)
  blocking collectives  292 us (27%)
  starting transfers between devices  53.7 us (5%)
  local copies, waits for them, and re-layouts  25.3 us (2%)
  other arithmetic  16.8 us (2%)
  between operations  16.3 us (1%)
  matrix products  14.6 us (1%)
    unnamed x7, waiting for transfers between devices  628 us
    psum x1, blocking collectives, shards(): head_total, table_total = lax.psum((head_shard, dense_table), 'lead')  118 us
    all_gather x3, blocking collectives, shards(): h_full = lax.all_gather(h_owned, 'lead', axis=0, tiled=True)  103 us
    psum x1, blocking collectives, shards(): lax.psum((weight_grad, bias_grad, film_stats), 'tile')  71 us
    ppermute x5, waiting for transfers between devices, extended(): after = lax.ppermute(leading, axis, down)  33.8 us
    ppermute x5, starting transfers between devices, extended(): before = lax.ppermute(last, axis, up)  25.2 us
  transfers between devices with their start and end apart: 17, of which 13 were waited for; matrix products, arithmetic and copies ran while one was open for 3% of the time, Pallas kernels for 0%

commit v1 on v0

v1 whole, which is shorter than its diff:
```python
import numpy as np
import jax
import jax.numpy as jnp
import ml_dtypes
from jax import lax
from jax.experimental import pallas as pl
from jax.experimental.pallas import tpu as pltpu
from jax.sharding import PartitionSpec as P

MESH = pl.DeviceIdType.MESH
BF = jnp.bfloat16
F32 = jnp.float32
L, T, HID, W = 32, 16, 384, 128
OWN, PAD, GATES, TAPS = 12, 16, 4, 9
GR = GATES * PAD
CP = L * PAD


def one_hots():
    a = np.zeros((TAPS * GR, OWN * TAPS * GATES), np.float32)
    pack = np.zeros((TAPS * GR, 512), np.float32)
    unpack = np.zeros((OWN * TAPS * GATES, 512), np.float32)
    for k in range(TAPS):
        for j in range(GATES):
            for o in range(OWN):
                inner = k * GR + j * PAD + o
                outer = (o * TAPS + k) * GATES + j
                column = k * 48 + j * OWN + o + (0 if k < 5 else 16)
                a[inner, outer] = 1
                pack[inner, column] = 1
                unpack[outer, column] = 1
    e = np.zeros((HID, CP), np.float32)
    for i in range(L):
        for o in range(OWN):
            e[i * OWN + o, i * PAD + o] = 1
    spread = np.zeros((512, HID), np.float32)
    for q in range(4):
        for c in range(96):
            spread[128 * q + c, 96 * q + c] = 1
    rows = np.zeros((2, 48, 32), np.float32)
    for half in range(2):
        for c in range(24):
            rows[half, 24 * half + c, (c // OWN) * PAD + c % OWN] = 1
    return [x.astype(ml_dtypes.bfloat16) for x in (a, pack, unpack, e, e.T.copy(), spread, rows)]


def nn(a, b):
    return lax.dot_general(a, b, (((1,), (0,)), ((), ())), preferred_element_type=F32)


def nt(a, b):
    return lax.dot_general(a, b, (((1,), (1,)), ((), ())), preferred_element_type=F32)


def shifted(x, s):
    if s == 0:
        return x
    lane = lax.broadcasted_iota(jnp.int32, x.shape, 1)
    keep = lane < W - s if s > 0 else lane >= -s
    return jnp.where(keep, pltpu.roll(x, (-s) % W, 1), 0.0)


def shifted_rows(x, s):
    if s == 0:
        return x
    row = lax.broadcasted_iota(jnp.int32, x.shape, 0)
    keep = row < W - s if s > 0 else row >= -s
    return jnp.where(keep, pltpu.roll(x, (-s) % W, 0), 0.0)


(S_YX0, S_YX1, S_YX2, S_H1, S_H2, S_H3, S_YH1, S_YH2, S_COTH, S_COTB, S_FR, S_HB1, S_HB2, S_DH3, S_DH2, S_DH1,
 S_V, S_ST, S_STL, S_DZN2, S_DZN1, S_DZN0, S_DZF2, S_DZF1, S_DZF0, S_BI, S_WH, S_WF, S_PR, S_PT, S_PL, NSEM) = range(32)


def kernel(
    frames, wsrc, bias, hw, film, idx, cot, a_ref, pack, unpack, e_ref, et_ref, spread, rsel,
    wg_out, bg_out, hg_out, fg_out,
    wx, whp, whpt, yx, yh, rx, rh, hbuf, coth, cot4, cotb, fsend, fblk, hblk, dv_ref, dhp, dhr,
    v4, vblk, st_send, st_tile, stl_send, stl, dz_send, dzbuf, bi_send, bi, stack, scat,
    wsend, wrecv, xf, cc, vv, pbuf, prec, psum, ptile, plead, ssem, rsem,
):
    li = lax.axis_index("lead")
    ti = lax.axis_index("tile")

    def lead_dev(to):
        return (to, ti)

    def tile_dev(to):
        return (li, to)

    def send(src, dst, sem, dev):
        pltpu.make_async_remote_copy(
            src_ref=src, dst_ref=dst, send_sem=ssem.at[sem], recv_sem=rsem.at[sem], device_id=dev, device_id_type=MESH
        ).start()

    def got(ref, sem):
        pltpu.make_async_copy(ref, ref, rsem.at[sem]).wait()

    def sent(ref, sem):
        pltpu.make_async_copy(ref, ref, ssem.at[sem]).wait()

    def each_lead(fn):
        def body(d, carry):
            fn(lax.rem(li + d, L))
            return carry
        lax.fori_loop(1, L, body, 0)

    def each_tile(fn, first=1, last=T):
        def body(d, carry):
            fn(lax.rem(ti + d, T))
            return carry
        lax.fori_loop(first, last, body, 0)

    bar = pltpu.get_barrier_semaphore()
    each_lead(lambda to: pl.semaphore_signal(bar, inc=1, device_id=lead_dev(to), device_id_type=MESH))
    each_tile(lambda to: pl.semaphore_signal(bar, inc=1, device_id=tile_dev(to), device_id_type=MESH))

    up = lax.rem(ti + 1, T)
    down = lax.rem(ti + T - 1, T)
    has_up = ti < T - 1
    has_down = ti > 0

    wt = nn(a_ref[...], wsrc[...]).astype(BF)
    wx[...] = wt[:, :HID]
    wth = wt[:, HID:]
    whp[...] = nn(wth, e_ref[...]).astype(BF)
    whpt[...] = nt(et_ref[...], wth).astype(BF)

    def row_parts(g):
        parts = []
        for a in range(3):
            total = None
            for b in range(3):
                k = 3 * a + b
                term = shifted(g[k * GR:(k + 1) * GR], b - 1)
                total = term if total is None else total + term
            parts.append(total)
        return parts

    for t in range(3):
        parts = row_parts(nn(wx[...], frames[t]))
        for a in range(3):
            yx[t, a] = parts[a]
    for t in range(3):
        fsend[:, t] = nn(et_ref[...], frames[t]).astype(BF).reshape(T, 2 * PAD, W)
    for p in range(4):
        cot4[p] = cot[96 * p:96 * (p + 1), :]
    stack[...] = jnp.zeros_like(stack)
    cc[...] = jnp.zeros_like(cc)
    vv[...] = jnp.zeros_like(vv)
    pbuf[...] = jnp.zeros_like(pbuf)

    pl.semaphore_wait(bar, L + T - 2)

    def halo(src, dst, sem):
        send(src.at[0], dst.at[0], sem, tile_dev(up))
        send(src.at[2], dst.at[1], sem, tile_dev(down))

    for t in range(3):
        halo(yx.at[t], rx.at[t], (S_YX0, S_YX1, S_YX2)[t])
    send(cot, coth.at[0], S_COTH, tile_dev(lax.rem(ti + 2, T)))
    send(cot, coth.at[1], S_COTH, tile_dev(lax.rem(ti + T - 2, T)))

    def from_neighbours(r):
        return jnp.where(has_down, r[0], 0.0) + jnp.where(has_up, r[1], 0.0)

    def cell(z, previous):
        i_g = jax.nn.sigmoid(z[0:PAD])
        f_g = jax.nn.sigmoid(z[PAD:2 * PAD])
        g_g = jnp.tanh(z[2 * PAD:3 * PAD])
        o_g = jax.nn.sigmoid(z[3 * PAD:4 * PAD])
        now = f_g * previous + i_g * g_g
        return (i_g, f_g, g_g, o_g, previous, now), (o_g * jnp.tanh(now)).astype(BF)

    def share_h(t, h):
        buf = hbuf.at[t]
        buf[li] = h
        sem = (S_H1, S_H2, S_H3)[t]
        each_lead(lambda to: send(buf.at[li], buf.at[li], sem, lead_dev(to)))

    def await_h(t):
        got(hbuf.at[t, pl.ds(0, L - 1)], (S_H1, S_H2, S_H3)[t])

    saved = []
    got(rx.at[0], S_YX0)
    z = yx[0, 1] + from_neighbours(rx.at[0]) + bias[...]
    state, h = cell(z, jnp.zeros((PAD, W), F32))
    saved.append(state)
    share_h(0, h)

    mine = lax.div(ti, 4)

    def send_cot(to):
        send(cot4.at[lax.div(to, 4)], cotb.at[ti], S_COTB, tile_dev(to))

    def send_frames(to):
        send(fsend.at[to], fblk.at[ti], S_FR, tile_dev(to))

    for t in (1, 2):
        await_h(t - 1)
        parts = row_parts(nn(whp[...], hbuf[t - 1].reshape(CP, W)))
        for a in (0, 2):
            yh[t - 1, a] = parts[a]
        sem = (S_YH1, S_YH2)[t - 1]
        halo(yh.at[t - 1], rh.at[t - 1], sem)
        hsem = (S_HB1, S_HB2)[t - 1]
        hb = hblk.at[t - 1]
        hs = hbuf.at[t - 1]
        hb[ti] = hs[pl.ds(2 * ti, 2)]
        each_tile(lambda to: send(hs.at[pl.ds(2 * to, 2)], hb.at[ti], hsem, tile_dev(to)))
        got(rx.at[t], (S_YX0, S_YX1, S_YX2)[t])
        base = yx[t, 1] + from_neighbours(rx.at[t]) + bias[...] + parts[1]
        got(rh.at[t - 1], sem)
        z = base + from_neighbours(rh.at[t - 1])
        state, h = cell(z, saved[-1][5])
        saved.append(state)
        share_h(t, h)
        if t == 1:
            each_tile(send_frames)
            fblk[ti] = fsend[ti]
            got(coth, S_COTH)
            zero = jnp.zeros((HID, W), BF)
            rows = (jnp.where(ti < T - 2, coth[1], zero), cot[...], jnp.where(ti >= 2, coth[0], zero))
            dvt = jnp.zeros((W, HID), F32)
            for a in range(3):
                ct = rows[a].astype(F32).T
                for b in range(3):
                    k = 3 * a + b
                    dvt = dvt + nn(shifted_rows(ct, -2 * (b - 1)).astype(BF), hw[k * HID:(k + 1) * HID, :])
            dv = dvt.T
            dv_ref[...] = jnp.zeros_like(dv_ref)
            for i in range(L):
                dv_ref[0, i, 0:OWN, :] = dv[i * OWN:(i + 1) * OWN]
            dv_ref[1] = nn(et_ref[...], cot[...]).reshape(L, PAD, W)
        else:
            each_tile(send_cot)
            cotb[ti] = cot4[mine]

    await_h(2)
    h_wide = hbuf[2].reshape(CP, W).astype(F32)
    gamma = 1.0 + film[:, 0:1]
    u = gamma * h_wide + film[:, 1:2]
    s = jax.nn.sigmoid(u)
    du = dv_ref[0].reshape(CP, W) * s * (1.0 + u * (1.0 - s))
    dhp[0] = (dv_ref[1].reshape(CP, W) + gamma * du).reshape(L, PAD, W)

    def share_dh(n):
        sem = (S_DH3, S_DH2, S_DH1)[n]
        src = dhp.at[n]
        dst = dhr.at[n]
        each_lead(lambda to: send(src.at[to], dst.at[li], sem, lead_dev(to)))
        dst[li] = src[li]

    def await_dh(n):
        got(dhr.at[n, pl.ds(0, L - 1)], (S_DH3, S_DH2, S_DH1)[n])
        return jnp.sum(dhr[n], axis=0)

    share_dh(0)
    v = nn(e_ref[...], (u * s).astype(BF)).astype(BF)
    for q in range(4):
        v4[q] = v[96 * q:96 * (q + 1)]
    each_tile(lambda to: send(v4.at[lax.rem(to, 4)], vblk.at[ti], S_V, tile_dev(to)))
    vblk[ti] = v4[lax.rem(ti, 4)]
    for n, field in enumerate((du * h_wide, du)):
        line = jnp.sum(field.T, axis=0, keepdims=True)
        for q in range(4):
            st_send[4 * n + q:4 * n + q + 1, :] = line[:, 128 * q:128 * (q + 1)]
    each_tile(lambda to: send(st_send, st_tile.at[ti], S_ST, tile_dev(to)))
    st_tile[ti] = st_send[...]

    bias_sum = jnp.zeros((GR, W), F32)
    dc = jnp.zeros((PAD, W), F32)

    def gate_grads(n, dh, dc):
        i_g, f_g, g_g, o_g, previous, now = saved[2 - n]
        sq = jnp.tanh(now)
        dc = dc + dh * o_g * (1.0 - sq * sq)
        dz = jnp.concatenate(
            [
                dc * g_g * i_g * (1.0 - i_g),
                dc * previous * f_g * (1.0 - f_g),
                dc * i_g * (1.0 - g_g * g_g),
                dh * sq * o_g * (1.0 - o_g),
            ],
            0,
        )
        src = dz_send.at[n]
        dst = dzbuf.at[n]
        src[...] = dz.astype(BF)
        near = (S_DZN2, S_DZN1, S_DZN0)[n]
        far = (S_DZF2, S_DZF1, S_DZF0)[n]
        for to in (up, down):
            send(src, dst.at[ti], near, tile_dev(to))
        each_tile(lambda to: send(src, dst.at[ti], far, tile_dev(to)), 2, T - 1)
        dst[ti] = src[...]
        return dz, dc * f_g

    def await_near(n):
        got(dzbuf.at[n, pl.ds(0, 2)], (S_DZN2, S_DZN1, S_DZN0)[n])

    def await_far(n):
        got(dzbuf.at[n, pl.ds(0, T - 3)], (S_DZF2, S_DZF1, S_DZF0)[n])

    def back(n):
        zero = jnp.zeros((GR, W), F32)
        rows = (
            jnp.where(has_up, dzbuf[n, up].astype(F32), zero),
            dzbuf[n, ti].astype(F32),
            jnp.where(has_down, dzbuf[n, down].astype(F32), zero),
        )
        pieces = [shifted(rows[a], 1 - b).astype(BF) for a in range(3) for b in range(3)]
        dhp[n + 1] = nn(whpt[...], jnp.concatenate(pieces, 0)).reshape(L, PAD, W)

    def weight_part(n):
        t = 2 - n
        src = dzbuf.at[n]

        def body(row, carry):
            block = src[row].astype(F32)
            for b in range(3):
                piece = shifted(block, 1 - b).astype(BF)
                for a in range(3):
                    k = 3 * a + b
                    at = pl.multiple_of((row + a) * W, W)
                    stack[k * GR:(k + 1) * GR, pl.ds(at, W)] = piece
            at = pl.multiple_of(row * W, W)
            scat[0:2 * PAD, pl.ds(at, W)] = fblk[row, t]
            if t > 0:
                scat[2 * PAD:4 * PAD, pl.ds(at, W)] = hblk[t - 1, row].reshape(2 * PAD, W)
            return carry

        lax.fori_loop(0, T, body, 0)
        stack[0:3 * GR, T * W:(T + 1) * W] = jnp.zeros((3 * GR, W), BF)
        stack[6 * GR:9 * GR, W:2 * W] = jnp.zeros((3 * GR, W), BF)
        rows = 4 * PAD if t > 0 else 2 * PAD
        return nt(scat[0:rows, :], stack[:, W:(T + 1) * W])

    def share_weights(n, x):
        sem = (S_WH, S_WF)[n]
        y = nn((x * (1.0 / 256.0)).astype(BF), pack[...]).astype(BF)
        wsend[n] = (nn(rsel[0], y[:, :256]) + nn(rsel[1], y[:, 256:])).astype(BF)
        src = wsend.at[n]
        dst = wrecv.at[n]
        each_tile(lambda to: send(src, dst.at[ti], sem, tile_dev(to)))
        dst[ti] = src[...]

    def finish_weights(n):
        got(wrecv.at[n, pl.ds(0, T - 1)], (S_WH, S_WF)[n])
        for s_ in range(T):
            block = wrecv[n, s_].astype(F32)
            xf[24 * s_:24 * (s_ + 1), 0:256] = block[0:24]
            xf[24 * s_:24 * (s_ + 1), 256:512] = block[24:48]
        out = nt(unpack[...], xf[...].astype(BF)).astype(BF)
        col = HID * (1 - n)
        wg_out[:, col:col + HID] = out

    dz, dc = gate_grads(0, await_dh(0), dc)
    bias_sum = bias_sum + dz
    await_near(0)
    back(0)
    share_dh(1)

    got(st_tile.at[pl.ds(0, T - 1)], S_ST)
    stl_send[0:8, :] = jnp.sum(st_tile[...], axis=0)
    lane = lax.broadcasted_iota(jnp.int32, (8, W), 1)
    stl_send[8:16, :] = jnp.where(lane == idx[...], 1.0, 0.0)
    each_lead(lambda to: send(stl_send, stl.at[li], S_STL, lead_dev(to)))
    stl[li] = stl_send[...]

    got(cotb.at[pl.ds(0, T - 1)], S_COTB)
    got(vblk.at[pl.ds(0, T - 1)], S_V)

    def head_rows(row, carry):
        block = cotb[row].astype(F32)
        at = pl.multiple_of((row + 2) * W, W)
        for b in range(3):
            cc[96 * b:96 * (b + 1), pl.ds(at, W)] = shifted(block, 2 * (1 - b)).astype(BF)
        vv[0:96, pl.ds(pl.multiple_of(row * W, W), W)] = vblk[row]
        return carry

    lax.fori_loop(0, T, head_rows, 0)
    for a in range(3):
        first = (4 - 2 * a) * W
        part = nt(cc[:, first:first + T * W], vv[...])
        for b in range(3):
            k = 3 * a + b
            for d in range(4):
                pbuf[d * 256 + k * 24:d * 256 + (k + 1) * 24, :] = part[b * 96 + d * 24:b * 96 + (d + 1) * 24]
    each_lead(lambda to: send(pbuf.at[pl.ds(pl.multiple_of(32 * to, 32), 32)], prec.at[li], S_PR, lead_dev(to)))
    prec[li] = pbuf[pl.ds(pl.multiple_of(32 * li, 32), 32), :]

    dz, dc = gate_grads(1, await_dh(1), dc)
    bias_sum = bias_sum + dz
    await_near(1)
    back(1)
    share_dh(2)

    await_far(0)
    got(fblk.at[pl.ds(0, T - 1)], S_FR)
    got(hblk.at[1, pl.ds(0, T - 1)], S_HB2)
    grads = weight_part(0)
    await_far(1)
    got(hblk.at[0, pl.ds(0, T - 1)], S_HB1)
    grads = grads + weight_part(1)
    share_weights(0, grads[2 * PAD:4 * PAD])

    dz, dc = gate_grads(2, await_dh(2), dc)
    bias_sum = bias_sum + dz
    column = jnp.sum(bias_sum, axis=1, keepdims=True)
    lane = lax.broadcasted_iota(jnp.int32, (GR, W), 1)
    sub = lax.broadcasted_iota(jnp.int32, (GR, W), 0)
    line = jnp.sum(jnp.where(lane == sub, column, 0.0), axis=0, keepdims=True)
    bi_send[...] = jnp.broadcast_to(line, (8, W))
    each_tile(lambda to: send(bi_send, bi.at[ti], S_BI, tile_dev(to)))
    bi[ti] = bi_send[...]

    got(prec.at[pl.ds(0, L - 1)], S_PR)
    psum[...] = (jnp.sum(prec[...], axis=0) * (1.0 / 256.0)).astype(BF)
    owner = mine * 4 + lax.div(li, 8)
    quarter = lax.rem(ti, 4)

    @pl.when(owner != ti)
    def _():
        send(psum, ptile.at[quarter], S_PT, tile_dev(owner))

    await_near(2)
    await_far(2)
    grads0 = weight_part(2)
    share_weights(1, grads[0:2 * PAD] + grads0)

    @pl.when(owner == ti)
    def _():
        ptile[quarter] = psum[...]
        got(ptile.at[pl.ds(0, 3)], S_PT)
        each_lead(lambda to: send(ptile, plead.at[lax.rem(li, 8)], S_PL, lead_dev(to)))
        plead[lax.rem(li, 8)] = ptile[...]

    got(stl.at[pl.ds(0, L - 1)], S_STL)

    def table(l, acc):
        block = stl[l]
        return tuple(acc[m] + block[8:16, m:m + 1] * block[0:8, :] for m in range(16))

    acc = lax.fori_loop(0, L, table, tuple(jnp.zeros((8, W), F32) for _ in range(16)))
    for m in range(16):
        fg_out[m] = acc[m] * (1.0 / 256.0)
    got(bi.at[pl.ds(0, T - 1)], S_BI)
    bg_out[...] = jnp.sum(bi[...], axis=0) * (1.0 / 256.0)
    finish_weights(0)

    @pl.when(owner == ti)
    def _():
        got(plead.at[pl.ds(0, 7)], S_PL)

    @pl.when(owner != ti)
    def _():
        got(plead, S_PL)

    wide = jnp.concatenate([plead[:, q].reshape(256, W) for q in range(4)], 1)
    hg_out[...] = nn(wide, spread[...])[0:TAPS * 24].astype(BF)
    finish_weights(1)

    for t in range(3):
        sent(rx.at[t], (S_YX0, S_YX1, S_YX2)[t])
        sent(hbuf.at[t, pl.ds(0, L - 1)], (S_H1, S_H2, S_H3)[t])
        sent(dhr.at[t, pl.ds(0, L - 1)], (S_DH3, S_DH2, S_DH1)[t])
        sent(dzbuf.at[t, pl.ds(0, 2)], (S_DZN2, S_DZN1, S_DZN0)[t])
        sent(dzbuf.at[t, pl.ds(0, T - 3)], (S_DZF2, S_DZF1, S_DZF0)[t])
    for t in range(2):
        sent(rh.at[t], (S_YH1, S_YH2)[t])
        sent(hblk.at[t, pl.ds(0, T - 1)], (S_HB1, S_HB2)[t])
        sent(wrecv.at[t, pl.ds(0, T - 1)], (S_WH, S_WF)[t])
    sent(coth, S_COTH)
    sent(cotb.at[pl.ds(0, T - 1)], S_COTB)
    sent(fblk.at[pl.ds(0, T - 1)], S_FR)
    sent(vblk.at[pl.ds(0, T - 1)], S_V)
    sent(st_tile.at[pl.ds(0, T - 1)], S_ST)
    sent(stl.at[pl.ds(0, L - 1)], S_STL)
    sent(bi.at[pl.ds(0, T - 1)], S_BI)
    sent(prec.at[pl.ds(0, L - 1)], S_PR)

    @pl.when(owner != ti)
    def _():
        sent(psum, S_PT)

    @pl.when(owner == ti)
    def _():
        def body(d, carry):
            sent(ptile, S_PL)
            return carry
        lax.fori_loop(1, L, body, 0)


def shards(frames, enc_weight, enc_bias, head_weight, film_table, lead_index, cotangent):
    consts = [jnp.asarray(x) for x in one_hots()]
    wsrc = enc_weight.transpose(0, 2, 1, 3).reshape(OWN * TAPS * GATES, 2 * HID)
    bias = jnp.pad(enc_bias.T, ((0, 0), (0, PAD - OWN))).reshape(GR, 1)
    bias = jnp.broadcast_to(bias, (GR, W))
    chosen = (jnp.arange(film_table.shape[0]) == lead_index[0]).astype(F32)
    film = jnp.sum(chosen[:, None, None] * film_table, 0)
    film = jnp.pad(film.reshape(2, L, OWN), ((0, 0), (0, 0), (0, PAD - OWN))).reshape(2, CP).T
    idx = jnp.broadcast_to(lead_index.reshape(1, 1), (8, W))
    hw = head_weight.transpose(1, 0, 2).reshape(TAPS * HID, HID)
    vm = pltpu.VMEM
    outs = pl.pallas_call(
        kernel,
        out_shape=(
            jax.ShapeDtypeStruct((OWN * TAPS * GATES, 2 * HID), BF),
            jax.ShapeDtypeStruct((8, W), F32),
            jax.ShapeDtypeStruct((TAPS * 24, HID), BF),
            jax.ShapeDtypeStruct((16, 8, W), F32),
        ),
        in_specs=[pl.BlockSpec(memory_space=vm)] * 14,
        out_specs=(pl.BlockSpec(memory_space=vm),) * 4,
        scratch_shapes=[
            vm((TAPS * GR, HID), BF),
            vm((TAPS * GR, CP), BF),
            vm((CP, TAPS * GR), BF),
            vm((3, 3, GR, W), F32),
            vm((2, 3, GR, W), F32),
            vm((3, 2, GR, W), F32),
            vm((2, 2, GR, W), F32),
            vm((3, L, PAD, W), BF),
            vm((2, HID, W), BF),
            vm((4, 96, W), BF),
            vm((T, 96, W), BF),
            vm((T, 3, 2 * PAD, W), BF),
            vm((T, 3, 2 * PAD, W), BF),
            vm((2, T, 2, PAD, W), BF),
            vm((2, L, PAD, W), F32),
            vm((3, L, PAD, W), F32),
            vm((3, L, PAD, W), F32),
            vm((4, 96, W), BF),
            vm((T, 96, W), BF),
            vm((8, W), F32),
            vm((T, 8, W), F32),
            vm((16, W), F32),
            vm((L, 16, W), F32),
            vm((3, GR, W), BF),
            vm((3, T, GR, W), BF),
            vm((8, W), F32),
            vm((T, 8, W), F32),
            vm((TAPS * GR, (T + 2) * W), BF),
            vm((4 * PAD, T * W), BF),
            vm((2, 48, 256), BF),
            vm((2, T, 48, 256), BF),
            vm((HID, 512), F32),
            vm((3 * 96, (T + 4) * W), BF),
            vm((W, T * W), BF),
            vm((L * 32, W), F32),
            vm((L, 32, W), F32),
            vm((32, W), BF),
            vm((4, 32, W), BF),
            vm((8, 4, 32, W), BF),
            pltpu.SemaphoreType.DMA((NSEM,)),
            pltpu.SemaphoreType.DMA((NSEM,)),
        ],
        compiler_params=pltpu.CompilerParams(
            collective_id=0, has_side_effects=True, vmem_limit_bytes=56 * 2**20
        ),
    )(frames.reshape(3, HID, W), wsrc, bias, hw, film, idx, cotangent.reshape(HID, W), *consts)
    wg, bg, hg, fg = outs
    wg = wg.reshape(OWN, TAPS, GATES, 2 * HID).transpose(0, 2, 1, 3)
    bg = bg[0, :GR].reshape(GATES, PAD)[:, :OWN].T
    hg = hg.reshape(TAPS, 24, HID).transpose(1, 0, 2)
    fg = fg.reshape(16, 2, L, PAD)[..., :OWN].reshape(16, 2, HID)
    return wg, bg, hg, fg


def solution(mesh):
    in_specs = (
        P(None, None, "tile", None),
        P("lead", None, None, None),
        P("lead", None),
        P(),
        P(),
        P("lead"),
        P("lead", None, "tile", None),
    )
    out_specs = (P("lead", None, None, None), P("lead", None), P("tile", None, None), P())
    return jax.shard_map(shards, mesh=mesh, in_specs=in_specs, out_specs=out_specs, check_vma=False)
```

time: 1100 us -> 176 us (0.16)
  waiting for transfers between devices: 681 us -> 0 us
  blocking collectives: 292 us -> 0 us
  Pallas kernels: 0 us -> 161 us
  starting transfers between devices: 53.7 us -> 0 us
  other arithmetic: 16.8 us -> 0.9 us
  between operations: 16.3 us -> 1.32 us
  matrix products: 14.6 us -> 0 us
  local copies, waits for them, and re-layouts: 25.3 us -> 12.6 us
    unnamed x7 -> x0, waiting for transfers between devices: 628 us -> none
    psum x2 -> x0, blocking collectives: 189 us -> none  [the longest x1 118 us: shards(): head_total, table_total = lax.psum((head_shard, dense_table), 'lead')]
    pallas_call x0 -> x1, Pallas kernels: none -> 161 us  [shards(): pl.pallas_call(kernel, out_shape=(jax.ShapeDtypeStruct((OWN * TAPS * GATE...]
    all_gather x3 -> x0, blocking collectives: 103 us -> none  [shards(): h_full = lax.all_gather(h_owned, 'lead', axis=0, tiled=True)]
    ppermute x12 -> x0, waiting for transfers between devices: 53.2 us -> none  [the longest x5 33.8 us: extended(): after = lax.ppermute(leading, axis, down)]
    ppermute x12 -> x0, starting transfers between devices: 44.3 us -> none  [the longest x5 25.2 us: extended(): before = lax.ppermute(last, axis, up)]
    dot_general x10 -> x0, matrix products: 14.6 us -> none  [the longest x3 10.1 us: shards(): jnp.einsum('ojrw,kcrw->ojkc', gate_low, fwd_taps, preferred_element_type=...]
    unnamed x166 -> x2, local copies, waits for them, and re-layouts: 14.7 us -> 1.91 us
  transfers between devices with their start and end apart: 17 -> 0, of which waited for: 13 -> 0; matrix products, arithmetic and copies ran while one was open for 3% -> 0% of each run, Pallas kernels for 0% -> 0%
where the time goes in v1:
time: 176 us; the launch traced here: 175 us
  Pallas kernels  161 us (91%)
  local copies, waits for them, and re-layouts  12.6 us (7%)
    pallas_call x1, Pallas kernels, shards(): pl.pallas_call(kernel, out_shape=(jax.ShapeDtypeStruct((OWN * TAPS * GATE...  161 us

profile of v1, /device:TPU:1, one launch (start us, length us, event | category | flops | bytes accessed | tf_op | source)
XLA Modules:
  0.0 175.4 jit_solution(4708017790136401674)
XLA Ops:
  1.3 0.7 pad.8
  2.0 0.1 broadcast_in_dim.6
  2.1 0.9 multiply_reduce_fusion
  3.0 0.6 broadcast_in_dim.15.idx
  3.6 0.1 reshape.50
  3.7 0.7 broadcast_in_dim.14.bias
  4.4 0.3 copy.22
  4.7 0.7 pad.9.clone
  5.4 2.2 %reshape.48.wsrc = bf16[432,768]{1,0:T(8,128)(2,1)} reshape(bf16[12,9,4,768]{3,2,1,0:T(4,128)(2,1)} %bitcast.25) | data formatting | bytes 1327104 | tf_op jit(solution)/shard_map/reshape | solution.py:496
  7.6 160.6 %shard_map.165 = (bf16[432,768]{1,0:T(8,128)(2,1)}, f32[8,128]{1,0:T(8,128)}, bf16[216,384]{1,0:T(8,128)(2,1)}, f32[16,8,128]{2,1,0:T(8,128)}) custom-call(bf16[3,384,128]{2,1,0:T(8,128)(2,1)} %bitcast.27, bf16[432,768]{1,0:T(8,128)(2,1)} %reshape.48.wsrc, f32[64,128]{1,0:T(8,128)} %broadcast_in_dim.14.bias, bf16[3456,384]{1,0:T(8,128)(2,1)} %bitcast.22, ...), custom_call_target="tpu_custom_call" | custom-call | tf_op jit(solution)/shard_map/pallas_call | solution.py:505
  168.2 2.3 %reshape.53 = bf16[12,9,4,768]{3,2,1,0:T(4,128)(2,1)} reshape(bf16[432,768]{1,0:T(8,128)(2,1)} %get-tuple-element.8) | data formatting | bytes 1327104 | tf_op jit(solution)/shard_map/reshape | solution.py:563
  170.5 0.7 slice_reduce_fusion
  171.2 0.1 reshape_squeeze.3
  171.2 0.6 slice_bitcast_fusion
  171.8 1.0 reshape.55
  172.9 1.0 reshape.57
  173.8 1.6 copy.25
  (1 shorter events, 0.0 us)

commit v2 on v1

--- a/solution.py
+++ b/solution.py
@@ -12,7 +12,7 @@
 F32 = jnp.float32
 L, T, HID, W = 32, 16, 384, 128
 OWN, PAD, GATES, TAPS = 12, 16, 4, 9
-GR = GATES * PAD
+GR = GATES * OWN
 CP = L * PAD
 
 
@@ -23,9 +23,9 @@
     for k in range(TAPS):
         for j in range(GATES):
             for o in range(OWN):
-                inner = k * GR + j * PAD + o
+                inner = k * GR + j * OWN + o
                 outer = (o * TAPS + k) * GATES + j
-                column = k * 48 + j * OWN + o + (0 if k < 5 else 16)
+                column = inner + (0 if k < 5 else 16)
                 a[inner, outer] = 1
                 pack[inner, column] = 1
                 unpack[outer, column] = 1
@@ -72,13 +72,19 @@
  S_V, S_ST, S_STL, S_DZN2, S_DZN1, S_DZN0, S_DZF2, S_DZF1, S_DZF0, S_BI, S_WH, S_WF, S_PR, S_PT, S_PL, NSEM) = range(32)
 
 
-def kernel(
-    frames, wsrc, bias, hw, film, idx, cot, a_ref, pack, unpack, e_ref, et_ref, spread, rsel,
-    wg_out, bg_out, hg_out, fg_out,
-    wx, whp, whpt, yx, yh, rx, rh, hbuf, coth, cot4, cotb, fsend, fblk, hblk, dv_ref, dhp, dhr,
-    v4, vblk, st_send, st_tile, stl_send, stl, dz_send, dzbuf, bi_send, bi, stack, scat,
-    wsend, wrecv, xf, cc, vv, pbuf, prec, psum, ptile, plead, ssem, rsem,
-):
+N_IN = 14
+
+
+def kernel(*refs):
+    inputs, (wg_out, bg_out, hg_out, fg_out), refs = refs[:N_IN], refs[N_IN:N_IN + 4], refs[N_IN + 4:]
+    held, refs = refs[:N_IN - 1], refs[N_IN - 1:]
+    idx = inputs[N_IN - 1]
+    (
+        wx, whp, whpt, yx, yh, rx, rh, hbuf, coth, cot4, cotb, fsend, fblk, hblk, dv_ref, dhp, dhr,
+        v4, vblk, st_send, st_tile, stl_send, stl, dz_send, dzbuf, bi_send, bi, stack, scat,
+        wsend, wrecv, xf, cc, vv, pbuf, psend, prec, psum, ptile, plead, film_col, flat, ssem, rsem, lsem,
+    ) = refs
+    wsrc, a_ref, frames, e_ref, et_ref, bias, film, cot, hw, pack, rsel, unpack, spread = held
     li = lax.axis_index("lead")
     ti = lax.axis_index("tile")
 
@@ -99,11 +105,33 @@
     def sent(ref, sem):
         pltpu.make_async_copy(ref, ref, ssem.at[sem]).wait()
 
+    def load(n):
+        return pltpu.make_async_copy(inputs[n], held[n], lsem.at[n])
+
     def each_lead(fn):
-        def body(d, carry):
-            fn(lax.rem(li + d, L))
+        ring, side, core = lax.rem(lax.div(li, 2), 8), lax.div(li, 16), lax.rem(li, 2)
+
+        def body(n, carry):
+            m = lax.div(n, 4)
+            step = lax.div(m + 1, 2) * (1 - 2 * lax.rem(m, 2))
+            other = lax.rem(ring + 12 + step, 8)
+            rest = 3 - lax.rem(n, 4)
+            side_to = lax.rem(side + lax.div(rest, 2), 2)
+            core_to = lax.rem(core + lax.rem(rest, 2), 2)
+            fn(side_to * 16 + other * 2 + core_to)
             return carry
-        lax.fori_loop(1, L, body, 0)
+        lax.fori_loop(0, L - 1, body, 0)
+
+    def each_tile_far_first(fn):
+        row, col = lax.div(ti, 4), lax.rem(ti, 4)
+
+        def away(m):
+            return 6 + lax.div(m + 1, 2) * (1 - 2 * lax.rem(m, 2))
+
+        def body(n, carry):
+            fn(lax.rem(row + away(lax.div(n, 4)), 4) * 4 + lax.rem(col + away(lax.rem(n, 4)), 4))
+            return carry
+        lax.fori_loop(0, T - 1, body, 0)
 
     def each_tile(fn, first=1, last=T):
         def body(d, carry):
@@ -113,13 +141,17 @@
 
     bar = pltpu.get_barrier_semaphore()
     each_lead(lambda to: pl.semaphore_signal(bar, inc=1, device_id=lead_dev(to), device_id_type=MESH))
-    each_tile(lambda to: pl.semaphore_signal(bar, inc=1, device_id=tile_dev(to), device_id_type=MESH))
+    each_tile_far_first(lambda to: pl.semaphore_signal(bar, inc=1, device_id=tile_dev(to), device_id_type=MESH))
+    for n in range(N_IN - 1):
+        load(n).start()
 
     up = lax.rem(ti + 1, T)
     down = lax.rem(ti + T - 1, T)
     has_up = ti < T - 1
     has_down = ti > 0
 
+    for n in range(5):
+        load(n).wait()
     wt = nn(a_ref[...], wsrc[...]).astype(BF)
     wx[...] = wt[:, :HID]
     wth = wt[:, HID:]
@@ -137,12 +169,25 @@
             parts.append(total)
         return parts
 
+    own_x = []
     for t in range(3):
         parts = row_parts(nn(wx[...], frames[t]))
-        for a in range(3):
-            yx[t, a] = parts[a]
+        for a in (0, 2):
+            yx[t, a] = parts[a].astype(BF)
+        own_x.append(parts[1])
     for t in range(3):
         fsend[:, t] = nn(et_ref[...], frames[t]).astype(BF).reshape(T, 2 * PAD, W)
+    for n in range(5, N_IN - 1):
+        load(n).wait()
+    sub = lax.broadcasted_iota(jnp.int32, (OWN, OWN), 0)
+    lane = lax.broadcasted_iota(jnp.int32, (OWN, OWN), 1)
+    bias_cols = [jnp.sum(jnp.where(sub == lane, bias[j:j + 1, :], 0.0), axis=1, keepdims=True) for j in range(GATES)]
+    slot = lax.broadcasted_iota(jnp.int32, (16, 2, HID), 0)
+    lines = jnp.sum(jnp.where(slot == idx[0], film[...], 0.0), axis=0)
+    lines = jnp.concatenate([lines, jnp.zeros((6, HID), F32)], 0).T
+    film_col[...] = jnp.zeros_like(film_col)
+    for i in range(L):
+        film_col[i, 0:OWN, :] = lines[i * OWN:(i + 1) * OWN]
     for p in range(4):
         cot4[p] = cot[96 * p:96 * (p + 1), :]
     stack[...] = jnp.zeros_like(stack)
@@ -158,17 +203,18 @@
 
     for t in range(3):
         halo(yx.at[t], rx.at[t], (S_YX0, S_YX1, S_YX2)[t])
-    send(cot, coth.at[0], S_COTH, tile_dev(lax.rem(ti + 2, T)))
-    send(cot, coth.at[1], S_COTH, tile_dev(lax.rem(ti + T - 2, T)))
-
     def from_neighbours(r):
-        return jnp.where(has_down, r[0], 0.0) + jnp.where(has_up, r[1], 0.0)
+        return jnp.where(has_down, r[0].astype(F32), 0.0) + jnp.where(has_up, r[1].astype(F32), 0.0)
+
+    def padded(x):
+        return jnp.concatenate([x, jnp.zeros((PAD - OWN, W), F32)], 0)
 
     def cell(z, previous):
-        i_g = jax.nn.sigmoid(z[0:PAD])
-        f_g = jax.nn.sigmoid(z[PAD:2 * PAD])
-        g_g = jnp.tanh(z[2 * PAD:3 * PAD])
-        o_g = jax.nn.sigmoid(z[3 * PAD:4 * PAD])
+        z = [padded(z[j * OWN:(j + 1) * OWN] + bias_cols[j]) for j in range(GATES)]
+        i_g = jax.nn.sigmoid(z[0])
+        f_g = jax.nn.sigmoid(z[1])
+        g_g = jnp.tanh(z[2])
+        o_g = jax.nn.sigmoid(z[3])
         now = f_g * previous + i_g * g_g
         return (i_g, f_g, g_g, o_g, previous, now), (o_g * jnp.tanh(now)).astype(BF)
 
@@ -183,10 +229,12 @@
 
     saved = []
     got(rx.at[0], S_YX0)
-    z = yx[0, 1] + from_neighbours(rx.at[0]) + bias[...]
+    z = own_x[0] + from_neighbours(rx.at[0])
     state, h = cell(z, jnp.zeros((PAD, W), F32))
     saved.append(state)
     share_h(0, h)
+    send(cot, coth.at[0], S_COTH, tile_dev(lax.rem(ti + 2, T)))
+    send(cot, coth.at[1], S_COTH, tile_dev(lax.rem(ti + T - 2, T)))
 
     mine = lax.div(ti, 4)
 
@@ -200,16 +248,11 @@
         await_h(t - 1)
         parts = row_parts(nn(whp[...], hbuf[t - 1].reshape(CP, W)))
         for a in (0, 2):
-            yh[t - 1, a] = parts[a]
+            yh[t - 1, a] = parts[a].astype(BF)
         sem = (S_YH1, S_YH2)[t - 1]
         halo(yh.at[t - 1], rh.at[t - 1], sem)
-        hsem = (S_HB1, S_HB2)[t - 1]
-        hb = hblk.at[t - 1]
-        hs = hbuf.at[t - 1]
-        hb[ti] = hs[pl.ds(2 * ti, 2)]
-        each_tile(lambda to: send(hs.at[pl.ds(2 * to, 2)], hb.at[ti], hsem, tile_dev(to)))
         got(rx.at[t], (S_YX0, S_YX1, S_YX2)[t])
-        base = yx[t, 1] + from_neighbours(rx.at[t]) + bias[...] + parts[1]
+        base = own_x[t] + from_neighbours(rx.at[t]) + parts[1]
         got(rh.at[t - 1], sem)
         z = base + from_neighbours(rh.at[t - 1])
         state, h = cell(z, saved[-1][5])
@@ -236,13 +279,21 @@
             each_tile(send_cot)
             cotb[ti] = cot4[mine]
 
+    def share_blocks(t):
+        hsem = (S_HB1, S_HB2)[t]
+        hb = hblk.at[t]
+        hs = hbuf.at[t]
+        hb[ti] = hs[pl.ds(2 * ti, 2)]
+        each_tile_far_first(lambda to: send(hs.at[pl.ds(2 * to, 2)], hb.at[ti], hsem, tile_dev(to)))
+
     await_h(2)
     h_wide = hbuf[2].reshape(CP, W).astype(F32)
-    gamma = 1.0 + film[:, 0:1]
-    u = gamma * h_wide + film[:, 1:2]
+    columns = film_col[...].reshape(CP, 8)
+    gamma = 1.0 + columns[:, 0:1]
+    u = gamma * h_wide + columns[:, 1:2]
     s = jax.nn.sigmoid(u)
     du = dv_ref[0].reshape(CP, W) * s * (1.0 + u * (1.0 - s))
-    dhp[0] = (dv_ref[1].reshape(CP, W) + gamma * du).reshape(L, PAD, W)
+    dhp[0] = (dv_ref[1].reshape(CP, W) + gamma * du).astype(BF).reshape(L, PAD, W)
 
     def share_dh(n):
         sem = (S_DH3, S_DH2, S_DH1)[n]
@@ -253,7 +304,7 @@
 
     def await_dh(n):
         got(dhr.at[n, pl.ds(0, L - 1)], (S_DH3, S_DH2, S_DH1)[n])
-        return jnp.sum(dhr[n], axis=0)
+        return jnp.sum(dhr[n].astype(F32), axis=0)
 
     share_dh(0)
     v = nn(e_ref[...], (u * s).astype(BF)).astype(BF)
@@ -261,10 +312,13 @@
         v4[q] = v[96 * q:96 * (q + 1)]
     each_tile(lambda to: send(v4.at[lax.rem(to, 4)], vblk.at[ti], S_V, tile_dev(to)))
     vblk[ti] = v4[lax.rem(ti, 4)]
+    st_send[...] = jnp.zeros_like(st_send)
     for n, field in enumerate((du * h_wide, du)):
-        line = jnp.sum(field.T, axis=0, keepdims=True)
-        for q in range(4):
-            st_send[4 * n + q:4 * n + q + 1, :] = line[:, 128 * q:128 * (q + 1)]
+        for i in range(L):
+            flat[i * OWN:(i + 1) * OWN, :] = field[i * PAD:i * PAD + OWN]
+        line = jnp.sum(flat[...].T, axis=0, keepdims=True)
+        for q in range(3):
+            st_send[3 * n + q:3 * n + q + 1, :] = line[:, 128 * q:128 * (q + 1)]
     each_tile(lambda to: send(st_send, st_tile.at[ti], S_ST, tile_dev(to)))
     st_tile[ti] = st_send[...]
 
@@ -276,12 +330,12 @@
         sq = jnp.tanh(now)
         dc = dc + dh * o_g * (1.0 - sq * sq)
         dz = jnp.concatenate(
-            [
+            [x[0:OWN] for x in (
                 dc * g_g * i_g * (1.0 - i_g),
                 dc * previous * f_g * (1.0 - f_g),
                 dc * i_g * (1.0 - g_g * g_g),
                 dh * sq * o_g * (1.0 - o_g),
-            ],
+            )],
             0,
         )
         src = dz_send.at[n]
@@ -289,17 +343,24 @@
         src[...] = dz.astype(BF)
         near = (S_DZN2, S_DZN1, S_DZN0)[n]
         far = (S_DZF2, S_DZF1, S_DZF0)[n]
-        for to in (up, down):
-            send(src, dst.at[ti], near, tile_dev(to))
-        each_tile(lambda to: send(src, dst.at[ti], far, tile_dev(to)), 2, T - 1)
         dst[ti] = src[...]
+        if n < 2:
+            for to in (up, down):
+                send(src, dst.at[ti], near, tile_dev(to))
+        else:
+            each_tile_far_first(lambda to: send(src, dst.at[ti], far, tile_dev(to)))
         return dz, dc * f_g
+
+    def share_far(n):
+        src = dz_send.at[n]
+        dst = dzbuf.at[n]
+        each_tile(lambda to: send(src, dst.at[ti], (S_DZF2, S_DZF1)[n], tile_dev(to)), 2, T - 1)
 
     def await_near(n):
         got(dzbuf.at[n, pl.ds(0, 2)], (S_DZN2, S_DZN1, S_DZN0)[n])
 
     def await_far(n):
-        got(dzbuf.at[n, pl.ds(0, T - 3)], (S_DZF2, S_DZF1, S_DZF0)[n])
+        got(dzbuf.at[n, pl.ds(0, T - 3 if n < 2 else T - 1)], (S_DZF2, S_DZF1, S_DZF0)[n])
 
     def back(n):
         zero = jnp.zeros((GR, W), F32)
@@ -309,7 +370,7 @@
             jnp.where(has_down, dzbuf[n, down].astype(F32), zero),
         )
         pieces = [shifted(rows[a], 1 - b).astype(BF) for a in range(3) for b in range(3)]
-        dhp[n + 1] = nn(whpt[...], jnp.concatenate(pieces, 0)).reshape(L, PAD, W)
+        dhp[n + 1] = nn(whpt[...], jnp.concatenate(pieces, 0)).astype(BF).reshape(L, PAD, W)
 
     def weight_part(n):
         t = 2 - n
@@ -359,11 +420,14 @@
     await_near(0)
     back(0)
     share_dh(1)
+    share_far(0)
+    share_blocks(1)
+    share_blocks(0)
 
     got(st_tile.at[pl.ds(0, T - 1)], S_ST)
     stl_send[0:8, :] = jnp.sum(st_tile[...], axis=0)
     lane = lax.broadcasted_iota(jnp.int32, (8, W), 1)
-    stl_send[8:16, :] = jnp.where(lane == idx[...], 1.0, 0.0)
+    stl_send[8:16, :] = jnp.where(lane == idx[0], 1.0, 0.0)
     each_lead(lambda to: send(stl_send, stl.at[li], S_STL, lead_dev(to)))
     stl[li] = stl_send[...]
 
@@ -386,14 +450,16 @@
             k = 3 * a + b
             for d in range(4):
                 pbuf[d * 256 + k * 24:d * 256 + (k + 1) * 24, :] = part[b * 96 + d * 24:b * 96 + (d + 1) * 24]
-    each_lead(lambda to: send(pbuf.at[pl.ds(pl.multiple_of(32 * to, 32), 32)], prec.at[li], S_PR, lead_dev(to)))
-    prec[li] = pbuf[pl.ds(pl.multiple_of(32 * li, 32), 32), :]
+    psend[...] = pbuf[...].astype(BF).reshape(L, 32, W)
+    each_lead(lambda to: send(psend.at[to], prec.at[li], S_PR, lead_dev(to)))
+    prec[li] = psend[li]
 
     dz, dc = gate_grads(1, await_dh(1), dc)
     bias_sum = bias_sum + dz
     await_near(1)
     back(1)
     share_dh(2)
+    share_far(1)
 
     await_far(0)
     got(fblk.at[pl.ds(0, T - 1)], S_FR)
@@ -415,7 +481,7 @@
     bi[ti] = bi_send[...]
 
     got(prec.at[pl.ds(0, L - 1)], S_PR)
-    psum[...] = (jnp.sum(prec[...], axis=0) * (1.0 / 256.0)).astype(BF)
+    psum[...] = (jnp.sum(prec[...].astype(F32), axis=0) * (1.0 / 256.0)).astype(BF)
     owner = mine * 4 + lax.div(li, 8)
     quarter = lax.rem(ti, 4)
 
@@ -423,7 +489,6 @@
     def _():
         send(psum, ptile.at[quarter], S_PT, tile_dev(owner))
 
-    await_near(2)
     await_far(2)
     grads0 = weight_part(2)
     share_weights(1, grads[0:2 * PAD] + grads0)
@@ -464,9 +529,10 @@
         sent(rx.at[t], (S_YX0, S_YX1, S_YX2)[t])
         sent(hbuf.at[t, pl.ds(0, L - 1)], (S_H1, S_H2, S_H3)[t])
         sent(dhr.at[t, pl.ds(0, L - 1)], (S_DH3, S_DH2, S_DH1)[t])
-        sent(dzbuf.at[t, pl.ds(0, 2)], (S_DZN2, S_DZN1, S_DZN0)[t])
-        sent(dzbuf.at[t, pl.ds(0, T - 3)], (S_DZF2, S_DZF1, S_DZF0)[t])
+    sent(dzbuf.at[2, pl.ds(0, T - 1)], S_DZF0)
     for t in range(2):
+        sent(dzbuf.at[t, pl.ds(0, 2)], (S_DZN2, S_DZN1)[t])
+        sent(dzbuf.at[t, pl.ds(0, T - 3)], (S_DZF2, S_DZF1)[t])
         sent(rh.at[t], (S_YH1, S_YH2)[t])
         sent(hblk.at[t, pl.ds(0, T - 1)], (S_HB1, S_HB2)[t])
         sent(wrecv.at[t, pl.ds(0, T - 1)], (S_WH, S_WF)[t])
@@ -491,17 +557,26 @@
         lax.fori_loop(1, L, body, 0)
 
 
+def finish(wg, bg, hg, fg, wg_out, bg_out, hg_out, fg_out):
+    wg_out[...] = wg[...].astype(F32).reshape(OWN, TAPS, GATES, 2 * HID).astype(BF)
+    hg_out[...] = hg[...]
+    for j in range(GATES):
+        bg_out[j:j + 1, :] = bg[0:1, j * OWN:(j + 1) * OWN]
+    for m in range(16):
+        for n in range(2):
+            for q in range(3):
+                fg_out[m, n:n + 1, W * q:W * (q + 1)] = fg[m, 3 * n + q:3 * n + q + 1, :]
+
+
 def shards(frames, enc_weight, enc_bias, head_weight, film_table, lead_index, cotangent):
-    consts = [jnp.asarray(x) for x in one_hots()]
+    a, pack, unpack, e, et, spread, rsel = [jnp.asarray(x) for x in one_hots()]
     wsrc = enc_weight.transpose(0, 2, 1, 3).reshape(OWN * TAPS * GATES, 2 * HID)
-    bias = jnp.pad(enc_bias.T, ((0, 0), (0, PAD - OWN))).reshape(GR, 1)
-    bias = jnp.broadcast_to(bias, (GR, W))
-    chosen = (jnp.arange(film_table.shape[0]) == lead_index[0]).astype(F32)
-    film = jnp.sum(chosen[:, None, None] * film_table, 0)
-    film = jnp.pad(film.reshape(2, L, OWN), ((0, 0), (0, 0), (0, PAD - OWN))).reshape(2, CP).T
-    idx = jnp.broadcast_to(lead_index.reshape(1, 1), (8, W))
     hw = head_weight.transpose(1, 0, 2).reshape(TAPS * HID, HID)
     vm = pltpu.VMEM
+    inputs = (
+        wsrc, a, frames.reshape(3, HID, W), e, et, enc_bias.T, film_table, cotangent.reshape(HID, W), hw, pack, rsel,
+        unpack, spread,
+    )
     outs = pl.pallas_call(
         kernel,
         out_shape=(
@@ -510,16 +585,16 @@
             jax.ShapeDtypeStruct((TAPS * 24, HID), BF),
             jax.ShapeDtypeStruct((16, 8, W), F32),
         ),
-        in_specs=[pl.BlockSpec(memory_space=vm)] * 14,
+        in_specs=[pl.BlockSpec(memory_space=pl.ANY)] * (N_IN - 1) + [pl.BlockSpec(memory_space=pltpu.SMEM)],
         out_specs=(pl.BlockSpec(memory_space=vm),) * 4,
-        scratch_shapes=[
+        scratch_shapes=[vm(x.shape, x.dtype) for x in inputs] + [
             vm((TAPS * GR, HID), BF),
             vm((TAPS * GR, CP), BF),
             vm((CP, TAPS * GR), BF),
-            vm((3, 3, GR, W), F32),
-            vm((2, 3, GR, W), F32),
-            vm((3, 2, GR, W), F32),
-            vm((2, 2, GR, W), F32),
+            vm((3, 3, GR, W), BF),
+            vm((2, 3, GR, W), BF),
+            vm((3, 2, GR, W), BF),
+            vm((2, 2, GR, W), BF),
             vm((3, L, PAD, W), BF),
             vm((2, HID, W), BF),
             vm((4, 96, W), BF),
@@ -528,8 +603,8 @@
             vm((T, 3, 2 * PAD, W), BF),
             vm((2, T, 2, PAD, W), BF),
             vm((2, L, PAD, W), F32),
-            vm((3, L, PAD, W), F32),
-            vm((3, L, PAD, W), F32),
+            vm((3, L, PAD, W), BF),
+            vm((3, L, PAD, W), BF),
             vm((4, 96, W), BF),
             vm((T, 96, W), BF),
             vm((8, W), F32),
@@ -548,23 +623,33 @@
             vm((3 * 96, (T + 4) * W), BF),
             vm((W, T * W), BF),
             vm((L * 32, W), F32),
-            vm((L, 32, W), F32),
+            vm((L, 32, W), BF),
+            vm((L, 32, W), BF),
             vm((32, W), BF),
             vm((4, 32, W), BF),
             vm((8, 4, 32, W), BF),
+            vm((L, PAD, 8), F32),
+            vm((HID, W), F32),
             pltpu.SemaphoreType.DMA((NSEM,)),
             pltpu.SemaphoreType.DMA((NSEM,)),
+            pltpu.SemaphoreType.DMA((N_IN - 1,)),
         ],
         compiler_params=pltpu.CompilerParams(
             collective_id=0, has_side_effects=True, vmem_limit_bytes=56 * 2**20
         ),
-    )(frames.reshape(3, HID, W), wsrc, bias, hw, film, idx, cotangent.reshape(HID, W), *consts)
-    wg, bg, hg, fg = outs
-    wg = wg.reshape(OWN, TAPS, GATES, 2 * HID).transpose(0, 2, 1, 3)
-    bg = bg[0, :GR].reshape(GATES, PAD)[:, :OWN].T
-    hg = hg.reshape(TAPS, 24, HID).transpose(1, 0, 2)
-    fg = fg.reshape(16, 2, L, PAD)[..., :OWN].reshape(16, 2, HID)
-    return wg, bg, hg, fg
+    )(*inputs, lead_index)
+    wg, bg, hg, fg = pl.pallas_call(
+        finish,
+        out_shape=(
+            jax.ShapeDtypeStruct((OWN, TAPS, GATES, 2 * HID), BF),
+            jax.ShapeDtypeStruct((GATES, OWN), F32),
+            jax.ShapeDtypeStruct((TAPS * 24, HID), BF),
+            jax.ShapeDtypeStruct((16, 2, HID), F32),
+        ),
+        in_specs=[pl.BlockSpec(memory_space=vm)] * 4,
+        out_specs=(pl.BlockSpec(memory_space=vm),) * 4,
+    )(*outs)
+    return wg.transpose(0, 2, 1, 3), bg.T, hg.reshape(TAPS, 24, HID).transpose(1, 0, 2), fg
 
 
 def solution(mesh):

time: 176 us -> 151 us (0.86)
  Pallas kernels: 161 us -> 147 us
  local copies, waits for them, and re-layouts: 12.6 us -> 2.21 us
    pallas_call x1, Pallas kernels: 161 us -> 145 us  [shards(): pl.pallas_call(kernel, out_shape=(jax.ShapeDtypeStruct((OWN * TAPS * GATE...]
    reshape x4 -> x0, local copies, waits for them, and re-layouts: 4.38 us -> none  [the longest x1 2.29 us: shards(): wg = wg.reshape(OWN, TAPS, GATES, 2 * HID).transpose(0, 2, 1, 3)]
    pallas_call x0 -> x1, Pallas kernels: none -> 2.36 us  [shards(): pl.pallas_call(finish, out_shape=(jax.ShapeDtypeStruct((OWN, TAPS, GATES,...]
    unnamed x2 -> x0, local copies, waits for them, and re-layouts: 1.91 us -> none
where the time goes in v2:
time: 151 us
  Pallas kernels  147 us (97%)
  local copies, waits for them, and re-layouts  2.21 us (1%)
    pallas_call x1, Pallas kernels, shards(): pl.pallas_call(kernel, out_shape=(jax.ShapeDtypeStruct((OWN * TAPS * GATE...  145 us

profile of v2, /device:TPU:1, one launch (start us, length us, event | category | flops | bytes accessed | tf_op | source)
XLA Modules:
  0.0 150.5 jit_solution(14065313318595980132)
XLA Ops:
  1.3 2.2 %reshape.23.refs_0_ = bf16[432,768]{1,0:T(8,128)(2,1)} reshape(bf16[12,9,4,768]{3,2,1,0:T(4,128)(2,1)} %bitcast.13) | data formatting | bytes 1327104 | tf_op jit(solution)/shard_map/reshape | solution.py:573
  3.5 144.7 %shard_map.165 = (bf16[432,768]{1,0:T(8,128)(2,1)}, f32[8,128]{1,0:T(8,128)}, bf16[216,384]{1,0:T(8,128)(2,1)}, f32[16,8,128]{2,1,0:T(8,128)}) custom-call(bf16[432,768]{1,0:T(8,128)(2,1)} %reshape.23.refs_0_, bf16[432,432]{1,0:T(8,128)(2,1)} %constant.14.clone.refs_1_, bf16[3,384,128]{2,1,0:T(8,128)(2,1)} %bitcast.14, ...), custom_call_target="tpu_custom_call" | custom-call | tf_op jit(solution)/shard_map/pallas_call | solution.py:580
  148.2 2.4 %shard_map.166 = (bf16[12,9,4,768]{3,2,1,0:T(4,128)(2,1)}, f32[4,12]{1,0:T(4,128)}, bf16[216,384]{1,0:T(8,128)(2,1)}, f32[16,2,384]{2,1,0:T(2,128)}) custom-call(bf16[432,768]{1,0:T(8,128)(2,1)} %get-tuple-element.12.wg, f32[8,128]{1,0:T(8,128)} %get-tuple-element.13.bg, bf16[216,384]{1,0:T(8,128)(2,1)} %get-tuple-element.14.hg, ...), custom_call_target="tpu_custom_call" | custom-call | tf_op jit(solution)/shard_map/pallas_call | solution.py:641

commit v3 on v2

--- a/solution.py
+++ b/solution.py
@@ -68,8 +68,9 @@
     return jnp.where(keep, pltpu.roll(x, (-s) % W, 0), 0.0)
 
 
-(S_YX0, S_YX1, S_YX2, S_H1, S_H2, S_H3, S_YH1, S_YH2, S_COTH, S_COTB, S_FR, S_HB1, S_HB2, S_DH3, S_DH2, S_DH1,
- S_V, S_ST, S_STL, S_DZN2, S_DZN1, S_DZN0, S_DZF2, S_DZF1, S_DZF0, S_BI, S_WH, S_WF, S_PR, S_PT, S_PL, NSEM) = range(32)
+(S_YX0, S_YX1, S_YX2, S_H1, S_H2, S_H3, S_YH1, S_YH2, S_COTH, S_COTZ, S_COTX, S_FR, S_FRC, S_HB1, S_HB2, S_HB1C, S_HB2C,
+ S_DH3, S_DH2, S_DH1, S_HQ, S_HQC, S_ST, S_STL, S_DZN2, S_DZN1, S_DZ0, S_DZZ2, S_DZZ1, S_DZX2, S_DZX1, S_BI, S_WHZ, S_WHX, S_WF,
+ S_PR, S_PT, S_PL, NSEM) = range(39)
 
 
 N_IN = 14
@@ -80,9 +81,9 @@
     held, refs = refs[:N_IN - 1], refs[N_IN - 1:]
     idx = inputs[N_IN - 1]
     (
-        wx, whp, whpt, yx, yh, rx, rh, hbuf, coth, cot4, cotb, fsend, fblk, hblk, dv_ref, dhp, dhr,
-        v4, vblk, st_send, st_tile, stl_send, stl, dz_send, dzbuf, bi_send, bi, stack, scat,
-        wsend, wrecv, xf, cc, vv, pbuf, psend, prec, psum, ptile, plead, film_col, flat, ssem, rsem, lsem,
+        wx, whp, whpt, yx, yh, rx, rh, hbuf, coth, cot4, cotz, cotb, fsend, fblk, hblk, dv_ref, dhp, dhr,
+        h8, hq, st_send, st_tile, stl_send, stl, dz_send, dznear, dzbuf, bi_send, bi, stack, scat,
+        wsend, wrecv, xf, cc, vv, pbuf, psend, prec, psum, ptile, plead, film_col, film_q, flat, ssem, rsem, lsem,
     ) = refs
     wsrc, a_ref, frames, e_ref, et_ref, bias, film, cot, hw, pack, rsel, unpack, spread = held
     li = lax.axis_index("lead")
@@ -109,7 +110,7 @@
         return pltpu.make_async_copy(inputs[n], held[n], lsem.at[n])
 
     def each_lead(fn):
-        ring, side, core = lax.rem(lax.div(li, 2), 8), lax.div(li, 16), lax.rem(li, 2)
+        ring, side = lax.rem(lax.div(li, 2), 8), lax.div(li, 16)
 
         def body(n, carry):
             m = lax.div(n, 4)
@@ -122,8 +123,19 @@
             return carry
         lax.fori_loop(0, L - 1, body, 0)
 
+    row, col = lax.div(ti, 4), lax.rem(ti, 4)
+    core = lax.rem(li, 2)
+    partner = lead_dev(li + 1 - 2 * core)
+
+    def each_z(fn):
+        for m in (2, 1, 3):
+            fn(lax.rem(col + m, 4))
+
+    def each_x(fn):
+        for m in (2, 1, 3):
+            fn(lax.rem(row + m, 4))
+
     def each_tile_far_first(fn):
-        row, col = lax.div(ti, 4), lax.rem(ti, 4)
 
         def away(m):
             return 6 + lax.div(m + 1, 2) * (1 - 2 * lax.rem(m, 2))
@@ -173,10 +185,10 @@
     for t in range(3):
         parts = row_parts(nn(wx[...], frames[t]))
         for a in (0, 2):
-            yx[t, a] = parts[a].astype(BF)
+            yx[t, a] = parts[a]
         own_x.append(parts[1])
     for t in range(3):
-        fsend[:, t] = nn(et_ref[...], frames[t]).astype(BF).reshape(T, 2 * PAD, W)
+        fsend[:, 2 * t:2 * t + 2] = nn(et_ref[...], frames[t]).astype(BF).reshape(T, 2, PAD, W)
     for n in range(5, N_IN - 1):
         load(n).wait()
     sub = lax.broadcasted_iota(jnp.int32, (OWN, OWN), 0)
@@ -188,6 +200,7 @@
     film_col[...] = jnp.zeros_like(film_col)
     for i in range(L):
         film_col[i, 0:OWN, :] = lines[i * OWN:(i + 1) * OWN]
+    film_q[...] = lines.reshape(4, 96, 8)
     for p in range(4):
         cot4[p] = cot[96 * p:96 * (p + 1), :]
     stack[...] = jnp.zeros_like(stack)
@@ -201,10 +214,9 @@
         send(src.at[0], dst.at[0], sem, tile_dev(up))
         send(src.at[2], dst.at[1], sem, tile_dev(down))
 
-    for t in range(3):
-        halo(yx.at[t], rx.at[t], (S_YX0, S_YX1, S_YX2)[t])
+    halo(yx.at[0], rx.at[0], S_YX0)
     def from_neighbours(r):
-        return jnp.where(has_down, r[0].astype(F32), 0.0) + jnp.where(has_up, r[1].astype(F32), 0.0)
+        return jnp.where(has_down, r[0], 0.0) + jnp.where(has_up, r[1], 0.0)
 
     def padded(x):
         return jnp.concatenate([x, jnp.zeros((PAD - OWN, W), F32)], 0)
@@ -233,22 +245,21 @@
     state, h = cell(z, jnp.zeros((PAD, W), F32))
     saved.append(state)
     share_h(0, h)
+    halo(yx.at[1], rx.at[1], S_YX1)
+    halo(yx.at[2], rx.at[2], S_YX2)
     send(cot, coth.at[0], S_COTH, tile_dev(lax.rem(ti + 2, T)))
-    send(cot, coth.at[1], S_COTH, tile_dev(lax.rem(ti + T - 2, T)))
-
-    mine = lax.div(ti, 4)
-
-    def send_cot(to):
-        send(cot4.at[lax.div(to, 4)], cotb.at[ti], S_COTB, tile_dev(to))
+
+    def half(x):
+        return x.at[pl.ds(3 * core, 3)]
 
     def send_frames(to):
-        send(fsend.at[to], fblk.at[ti], S_FR, tile_dev(to))
+        send(half(fsend.at[to]), half(fblk.at[ti]), S_FR, tile_dev(to))
 
     for t in (1, 2):
         await_h(t - 1)
         parts = row_parts(nn(whp[...], hbuf[t - 1].reshape(CP, W)))
         for a in (0, 2):
-            yh[t - 1, a] = parts[a].astype(BF)
+            yh[t - 1, a] = parts[a]
         sem = (S_YH1, S_YH2)[t - 1]
         halo(yh.at[t - 1], rh.at[t - 1], sem)
         got(rx.at[t], (S_YX0, S_YX1, S_YX2)[t])
@@ -259,32 +270,40 @@
         saved.append(state)
         share_h(t, h)
         if t == 1:
-            each_tile(send_frames)
-            fblk[ti] = fsend[ti]
-            got(coth, S_COTH)
-            zero = jnp.zeros((HID, W), BF)
-            rows = (jnp.where(ti < T - 2, coth[1], zero), cot[...], jnp.where(ti >= 2, coth[0], zero))
-            dvt = jnp.zeros((W, HID), F32)
-            for a in range(3):
-                ct = rows[a].astype(F32).T
-                for b in range(3):
-                    k = 3 * a + b
-                    dvt = dvt + nn(shifted_rows(ct, -2 * (b - 1)).astype(BF), hw[k * HID:(k + 1) * HID, :])
-            dv = dvt.T
-            dv_ref[...] = jnp.zeros_like(dv_ref)
-            for i in range(L):
-                dv_ref[0, i, 0:OWN, :] = dv[i * OWN:(i + 1) * OWN]
-            dv_ref[1] = nn(et_ref[...], cot[...]).reshape(L, PAD, W)
-        else:
-            each_tile(send_cot)
-            cotb[ti] = cot4[mine]
+            send(cot, coth.at[1], S_COTH, tile_dev(lax.rem(ti + T - 2, T)))
+    each_tile_far_first(send_frames)
+    fblk[ti, pl.ds(3 * core, 3)] = fsend[ti, pl.ds(3 * core, 3)]
+    each_z(lambda to: send(cot4.at[to], cotz.at[col], S_COTZ, tile_dev(row * 4 + to)))
+    cotz[col] = cot4[col]
+    got(coth, S_COTH)
+    zero = jnp.zeros((HID, W), BF)
+    rows = (jnp.where(ti < T - 2, coth[1], zero), cot[...], jnp.where(ti >= 2, coth[0], zero))
+    dvt = jnp.zeros((W, HID), F32)
+    for a in range(3):
+        ct = rows[a].astype(F32).T
+        for b in range(3):
+            k = 3 * a + b
+            dvt = dvt + nn(shifted_rows(ct, -2 * (b - 1)).astype(BF), hw[k * HID:(k + 1) * HID, :])
+    dv = dvt.T
+    dv_ref[...] = jnp.zeros_like(dv_ref)
+    for i in range(L):
+        dv_ref[0, i, 0:OWN, :] = dv[i * OWN:(i + 1) * OWN]
+    dv_ref[1] = nn(et_ref[...], cot[...]).reshape(L, PAD, W)
 
     def share_blocks(t):
         hsem = (S_HB1, S_HB2)[t]
         hb = hblk.at[t]
         hs = hbuf.at[t]
-        hb[ti] = hs[pl.ds(2 * ti, 2)]
-        each_tile_far_first(lambda to: send(hs.at[pl.ds(2 * to, 2)], hb.at[ti], hsem, tile_dev(to)))
+        hb[ti, core] = hs[2 * ti + core]
+        each_tile_far_first(lambda to: send(hs.at[2 * to + core], hb.at[ti, core], hsem, tile_dev(to)))
+
+    def swap_blocks(t):
+        got(hblk.at[t, pl.ds(0, T - 1), 0], (S_HB1, S_HB2)[t])
+        mine = hblk.at[t, :, core]
+        send(mine, mine, (S_HB1C, S_HB2C)[t], partner)
+
+    def await_blocks(t):
+        got(hblk.at[t, :, 0], (S_HB1C, S_HB2C)[t])
 
     await_h(2)
     h_wide = hbuf[2].reshape(CP, W).astype(F32)
@@ -307,11 +326,12 @@
         return jnp.sum(dhr[n].astype(F32), axis=0)
 
     share_dh(0)
-    v = nn(e_ref[...], (u * s).astype(BF)).astype(BF)
-    for q in range(4):
-        v4[q] = v[96 * q:96 * (q + 1)]
-    each_tile(lambda to: send(v4.at[lax.rem(to, 4)], vblk.at[ti], S_V, tile_dev(to)))
-    vblk[ti] = v4[lax.rem(ti, 4)]
+    h8[...] = nn(e_ref[...], hbuf[2].reshape(CP, W)).astype(BF).reshape(8, 48, W)
+    each_tile_far_first(lambda to: send(h8.at[2 * lax.div(to, 4) + core], hq.at[ti, core], S_HQ, tile_dev(to)))
+    hq[ti, core] = h8[2 * row + core]
+    got(cotz.at[pl.ds(0, 3)], S_COTZ)
+    each_x(lambda to: send(cotz, cotb.at[pl.ds(4 * row, 4)], S_COTX, tile_dev(to * 4 + col)))
+    cotb[pl.ds(4 * row, 4)] = cotz[...]
     st_send[...] = jnp.zeros_like(st_send)
     for n, field in enumerate((du * h_wide, du)):
         for i in range(L):
@@ -319,8 +339,11 @@
         line = jnp.sum(flat[...].T, axis=0, keepdims=True)
         for q in range(3):
             st_send[3 * n + q:3 * n + q + 1, :] = line[:, 128 * q:128 * (q + 1)]
-    each_tile(lambda to: send(st_send, st_tile.at[ti], S_ST, tile_dev(to)))
+    each_tile_far_first(lambda to: send(st_send, st_tile.at[ti], S_ST, tile_dev(to)))
     st_tile[ti] = st_send[...]
+    got(fblk.at[pl.ds(0, T - 1), pl.ds(0, 3)], S_FR)
+    fr_mine = fblk.at[:, pl.ds(3 * core, 3)]
+    send(fr_mine, fr_mine, S_FRC, partner)
 
     bias_sum = jnp.zeros((GR, W), F32)
     dc = jnp.zeros((PAD, W), F32)
@@ -341,33 +364,34 @@
         src = dz_send.at[n]
         dst = dzbuf.at[n]
         src[...] = dz.astype(BF)
-        near = (S_DZN2, S_DZN1, S_DZN0)[n]
-        far = (S_DZF2, S_DZF1, S_DZF0)[n]
         dst[ti] = src[...]
         if n < 2:
-            for to in (up, down):
-                send(src, dst.at[ti], near, tile_dev(to))
+            send(src, dznear.at[n, 0], (S_DZN2, S_DZN1)[n], tile_dev(up))
+            send(src, dznear.at[n, 1], (S_DZN2, S_DZN1)[n], tile_dev(down))
         else:
-            each_tile_far_first(lambda to: send(src, dst.at[ti], far, tile_dev(to)))
+            each_tile_far_first(lambda to: send(src, dst.at[ti], S_DZ0, tile_dev(to)))
         return dz, dc * f_g
 
-    def share_far(n):
-        src = dz_send.at[n]
-        dst = dzbuf.at[n]
-        each_tile(lambda to: send(src, dst.at[ti], (S_DZF2, S_DZF1)[n], tile_dev(to)), 2, T - 1)
-
     def await_near(n):
-        got(dzbuf.at[n, pl.ds(0, 2)], (S_DZN2, S_DZN1, S_DZN0)[n])
-
-    def await_far(n):
-        got(dzbuf.at[n, pl.ds(0, T - 3 if n < 2 else T - 1)], (S_DZF2, S_DZF1, S_DZF0)[n])
+        got(dznear.at[n], (S_DZN2, S_DZN1)[n])
+
+    def share_z(n):
+        each_z(lambda to: send(dz_send.at[n], dzbuf.at[n, ti], (S_DZZ2, S_DZZ1)[n], tile_dev(row * 4 + to)))
+
+    def share_x(n):
+        got(dzbuf.at[n, pl.ds(0, 3)], (S_DZZ2, S_DZZ1)[n])
+        mine = dzbuf.at[n, pl.ds(4 * row, 4)]
+        each_x(lambda to: send(mine, mine, (S_DZX2, S_DZX1)[n], tile_dev(to * 4 + col)))
+
+    def await_x(n):
+        got(dzbuf.at[n, pl.ds(0, 12)], (S_DZX2, S_DZX1)[n])
 
     def back(n):
         zero = jnp.zeros((GR, W), F32)
         rows = (
-            jnp.where(has_up, dzbuf[n, up].astype(F32), zero),
-            dzbuf[n, ti].astype(F32),
-            jnp.where(has_down, dzbuf[n, down].astype(F32), zero),
+            jnp.where(has_up, dznear[n, 1].astype(F32), zero),
+            dz_send[n].astype(F32),
+            jnp.where(has_down, dznear[n, 0].astype(F32), zero),
         )
         pieces = [shifted(rows[a], 1 - b).astype(BF) for a in range(3) for b in range(3)]
         dhp[n + 1] = nn(whpt[...], jnp.concatenate(pieces, 0)).astype(BF).reshape(L, PAD, W)
@@ -385,7 +409,7 @@
                     at = pl.multiple_of((row + a) * W, W)
                     stack[k * GR:(k + 1) * GR, pl.ds(at, W)] = piece
             at = pl.multiple_of(row * W, W)
-            scat[0:2 * PAD, pl.ds(at, W)] = fblk[row, t]
+            scat[0:2 * PAD, pl.ds(at, W)] = fblk[row, 2 * t:2 * t + 2].reshape(2 * PAD, W)
             if t > 0:
                 scat[2 * PAD:4 * PAD, pl.ds(at, W)] = hblk[t - 1, row].reshape(2 * PAD, W)
             return carry
@@ -397,16 +421,26 @@
         return nt(scat[0:rows, :], stack[:, W:(T + 1) * W])
 
     def share_weights(n, x):
-        sem = (S_WH, S_WF)[n]
         y = nn((x * (1.0 / 256.0)).astype(BF), pack[...]).astype(BF)
         wsend[n] = (nn(rsel[0], y[:, :256]) + nn(rsel[1], y[:, 256:])).astype(BF)
         src = wsend.at[n]
         dst = wrecv.at[n]
-        each_tile(lambda to: send(src, dst.at[ti], sem, tile_dev(to)))
         dst[ti] = src[...]
+        if n == 0:
+            each_z(lambda to: send(src, dst.at[ti], S_WHZ, tile_dev(row * 4 + to)))
+        else:
+            each_tile_far_first(lambda to: send(src, dst.at[ti], S_WF, tile_dev(to)))
+
+    def share_weights_x():
+        got(wrecv.at[0, pl.ds(0, 3)], S_WHZ)
+        mine = wrecv.at[0, pl.ds(4 * row, 4)]
+        each_x(lambda to: send(mine, mine, S_WHX, tile_dev(to * 4 + col)))
 
     def finish_weights(n):
-        got(wrecv.at[n, pl.ds(0, T - 1)], (S_WH, S_WF)[n])
+        if n == 0:
+            got(wrecv.at[0, pl.ds(0, 12)], S_WHX)
+        else:
+            got(wrecv.at[1, pl.ds(0, T - 1)], S_WF)
         for s_ in range(T):
             block = wrecv[n, s_].astype(F32)
             xf[24 * s_:24 * (s_ + 1), 0:256] = block[0:24]
@@ -420,9 +454,13 @@
     await_near(0)
     back(0)
     share_dh(1)
-    share_far(0)
+    share_z(0)
+    got(hq.at[pl.ds(0, T - 1), 0], S_HQ)
+    hq_mine = hq.at[:, core]
+    send(hq_mine, hq_mine, S_HQC, partner)
     share_blocks(1)
     share_blocks(0)
+    share_x(0)
 
     got(st_tile.at[pl.ds(0, T - 1)], S_ST)
     stl_send[0:8, :] = jnp.sum(st_tile[...], axis=0)
@@ -431,15 +469,18 @@
     each_lead(lambda to: send(stl_send, stl.at[li], S_STL, lead_dev(to)))
     stl[li] = stl_send[...]
 
-    got(cotb.at[pl.ds(0, T - 1)], S_COTB)
-    got(vblk.at[pl.ds(0, T - 1)], S_V)
-
-    def head_rows(row, carry):
-        block = cotb[row].astype(F32)
-        at = pl.multiple_of((row + 2) * W, W)
+    got(hq.at[:, 0], S_HQC)
+    got(cotb.at[pl.ds(0, 12)], S_COTX)
+    gamma_q = 1.0 + film_q[row, :, 0:1]
+    beta_q = film_q[row, :, 1:2]
+
+    def head_rows(r, carry):
+        block = cotb[r].astype(F32)
+        at = pl.multiple_of((r + 2) * W, W)
         for b in range(3):
             cc[96 * b:96 * (b + 1), pl.ds(at, W)] = shifted(block, 2 * (1 - b)).astype(BF)
-        vv[0:96, pl.ds(pl.multiple_of(row * W, W), W)] = vblk[row]
+        uq = gamma_q * hq[r].reshape(96, W).astype(F32) + beta_q
+        vv[0:96, pl.ds(pl.multiple_of(r * W, W), W)] = (uq * jax.nn.sigmoid(uq)).astype(BF)
         return carry
 
     lax.fori_loop(0, T, head_rows, 0)
@@ -451,7 +492,6 @@
             for d in range(4):
                 pbuf[d * 256 + k * 24:d * 256 + (k + 1) * 24, :] = part[b * 96 + d * 24:b * 96 + (d + 1) * 24]
     psend[...] = pbuf[...].astype(BF).reshape(L, 32, W)
-    each_lead(lambda to: send(psend.at[to], prec.at[li], S_PR, lead_dev(to)))
     prec[li] = psend[li]
 
     dz, dc = gate_grads(1, await_dh(1), dc)
@@ -459,44 +499,58 @@
     await_near(1)
     back(1)
     share_dh(2)
-    share_far(1)
-
-    await_far(0)
-    got(fblk.at[pl.ds(0, T - 1)], S_FR)
-    got(hblk.at[1, pl.ds(0, T - 1)], S_HB2)
+    share_z(1)
+    each_lead(lambda to: send(psend.at[to], prec.at[li], S_PR, lead_dev(to)))
+    swap_blocks(1)
+    swap_blocks(0)
+    share_x(1)
+    await_x(0)
+    got(fblk.at[:, pl.ds(0, 3)], S_FRC)
+    await_blocks(1)
     grads = weight_part(0)
-    await_far(1)
-    got(hblk.at[0, pl.ds(0, T - 1)], S_HB1)
+
+    dz, dc = gate_grads(2, await_dh(2), dc)
+    await_x(1)
+    await_blocks(0)
     grads = grads + weight_part(1)
     share_weights(0, grads[2 * PAD:4 * PAD])
-
-    dz, dc = gate_grads(2, await_dh(2), dc)
     bias_sum = bias_sum + dz
     column = jnp.sum(bias_sum, axis=1, keepdims=True)
     lane = lax.broadcasted_iota(jnp.int32, (GR, W), 1)
     sub = lax.broadcasted_iota(jnp.int32, (GR, W), 0)
     line = jnp.sum(jnp.where(lane == sub, column, 0.0), axis=0, keepdims=True)
     bi_send[...] = jnp.broadcast_to(line, (8, W))
-    each_tile(lambda to: send(bi_send, bi.at[ti], S_BI, tile_dev(to)))
+    each_tile_far_first(lambda to: send(bi_send, bi.at[ti], S_BI, tile_dev(to)))
     bi[ti] = bi_send[...]
 
     got(prec.at[pl.ds(0, L - 1)], S_PR)
     psum[...] = (jnp.sum(prec[...].astype(F32), axis=0) * (1.0 / 256.0)).astype(BF)
-    owner = mine * 4 + lax.div(li, 8)
-    quarter = lax.rem(ti, 4)
+    owner = col * 4 + lax.div(li, 8)
+    gathers = lax.div(li, 8) == col
 
     @pl.when(owner != ti)
     def _():
-        send(psum, ptile.at[quarter], S_PT, tile_dev(owner))
-
-    await_far(2)
+        send(psum, ptile.at[row], S_PT, tile_dev(owner))
+
+    @pl.when(owner == ti)
+    def _():
+        ptile[row] = psum[...]
+
+    got(dzbuf.at[2, pl.ds(0, T - 1)], S_DZ0)
     grads0 = weight_part(2)
     share_weights(1, grads[0:2 * PAD] + grads0)
-
-    @pl.when(owner == ti)
+    share_weights_x()
+
+    @pl.when(gathers)
     def _():
-        ptile[quarter] = psum[...]
-        got(ptile.at[pl.ds(0, 3)], S_PT)
+        @pl.when(owner == ti)
+        def _():
+            got(ptile.at[pl.ds(0, 3)], S_PT)
+
+        @pl.when(owner != ti)
+        def _():
+            got(ptile, S_PT)
+
         each_lead(lambda to: send(ptile, plead.at[lax.rem(li, 8)], S_PL, lead_dev(to)))
         plead[lax.rem(li, 8)] = ptile[...]
 
@@ -513,11 +567,11 @@
     bg_out[...] = jnp.sum(bi[...], axis=0) * (1.0 / 256.0)
     finish_weights(0)
 
-    @pl.when(owner == ti)
+    @pl.when(gathers)
     def _():
         got(plead.at[pl.ds(0, 7)], S_PL)
 
-    @pl.when(owner != ti)
+    @pl.when(jnp.logical_not(gathers))
     def _():
         got(plead, S_PL)
 
@@ -529,17 +583,24 @@
         sent(rx.at[t], (S_YX0, S_YX1, S_YX2)[t])
         sent(hbuf.at[t, pl.ds(0, L - 1)], (S_H1, S_H2, S_H3)[t])
         sent(dhr.at[t, pl.ds(0, L - 1)], (S_DH3, S_DH2, S_DH1)[t])
-    sent(dzbuf.at[2, pl.ds(0, T - 1)], S_DZF0)
     for t in range(2):
-        sent(dzbuf.at[t, pl.ds(0, 2)], (S_DZN2, S_DZN1)[t])
-        sent(dzbuf.at[t, pl.ds(0, T - 3)], (S_DZF2, S_DZF1)[t])
         sent(rh.at[t], (S_YH1, S_YH2)[t])
-        sent(hblk.at[t, pl.ds(0, T - 1)], (S_HB1, S_HB2)[t])
-        sent(wrecv.at[t, pl.ds(0, T - 1)], (S_WH, S_WF)[t])
+        sent(dznear.at[t], (S_DZN2, S_DZN1)[t])
+        sent(dzbuf.at[t, pl.ds(0, 3)], (S_DZZ2, S_DZZ1)[t])
+        sent(dzbuf.at[t, pl.ds(0, 12)], (S_DZX2, S_DZX1)[t])
+        sent(hblk.at[t, pl.ds(0, T - 1), 0], (S_HB1, S_HB2)[t])
+        sent(hblk.at[t, :, 0], (S_HB1C, S_HB2C)[t])
+    sent(dzbuf.at[2, pl.ds(0, T - 1)], S_DZ0)
+    sent(wrecv.at[0, pl.ds(0, 3)], S_WHZ)
+    sent(wrecv.at[0, pl.ds(0, 12)], S_WHX)
+    sent(wrecv.at[1, pl.ds(0, T - 1)], S_WF)
     sent(coth, S_COTH)
-    sent(cotb.at[pl.ds(0, T - 1)], S_COTB)
-    sent(fblk.at[pl.ds(0, T - 1)], S_FR)
-    sent(vblk.at[pl.ds(0, T - 1)], S_V)
+    sent(cotz.at[pl.ds(0, 3)], S_COTZ)
+    sent(cotb.at[pl.ds(0, 12)], S_COTX)
+    sent(fblk.at[pl.ds(0, T - 1), pl.ds(0, 3)], S_FR)
+    sent(fblk.at[:, pl.ds(0, 3)], S_FRC)
+    sent(hq.at[pl.ds(0, T - 1), 0], S_HQ)
+    sent(hq.at[:, 0], S_HQC)
     sent(st_tile.at[pl.ds(0, T - 1)], S_ST)
     sent(stl.at[pl.ds(0, L - 1)], S_STL)
     sent(bi.at[pl.ds(0, T - 1)], S_BI)
@@ -549,7 +610,7 @@
     def _():
         sent(psum, S_PT)
 
-    @pl.when(owner == ti)
+    @pl.when(gathers)
     def _():
         def body(d, carry):
             sent(ptile, S_PL)
@@ -591,27 +652,29 @@
             vm((TAPS * GR, HID), BF),
             vm((TAPS * GR, CP), BF),
             vm((CP, TAPS * GR), BF),
-            vm((3, 3, GR, W), BF),
-            vm((2, 3, GR, W), BF),
-            vm((3, 2, GR, W), BF),
-            vm((2, 2, GR, W), BF),
+            vm((3, 3, GR, W), F32),
+            vm((2, 3, GR, W), F32),
+            vm((3, 2, GR, W), F32),
+            vm((2, 2, GR, W), F32),
             vm((3, L, PAD, W), BF),
             vm((2, HID, W), BF),
             vm((4, 96, W), BF),
+            vm((4, 96, W), BF),
             vm((T, 96, W), BF),
-            vm((T, 3, 2 * PAD, W), BF),
-            vm((T, 3, 2 * PAD, W), BF),
+            vm((T, 6, PAD, W), BF),
+            vm((T, 6, PAD, W), BF),
             vm((2, T, 2, PAD, W), BF),
             vm((2, L, PAD, W), F32),
             vm((3, L, PAD, W), BF),
             vm((3, L, PAD, W), BF),
-            vm((4, 96, W), BF),
-            vm((T, 96, W), BF),
+            vm((8, 48, W), BF),
+            vm((T, 2, 48, W), BF),
             vm((8, W), F32),
             vm((T, 8, W), F32),
             vm((16, W), F32),
             vm((L, 16, W), F32),
             vm((3, GR, W), BF),
+            vm((2, 2, GR, W), BF),
             vm((3, T, GR, W), BF),
             vm((8, W), F32),
             vm((T, 8, W), F32),
@@ -629,6 +692,7 @@
             vm((4, 32, W), BF),
             vm((8, 4, 32, W), BF),
             vm((L, PAD, 8), F32),
+            vm((4, 96, 8), F32),
             vm((HID, W), F32),
             pltpu.SemaphoreType.DMA((NSEM,)),
             pltpu.SemaphoreType.DMA((NSEM,)),

time: 151 us -> 128 us (0.85)
  Pallas kernels: 147 us -> 125 us
    pallas_call x1, Pallas kernels: 145 us -> 122 us  [shards(): pl.pallas_call(kernel, out_shape=(jax.ShapeDtypeStruct((OWN * TAPS * GATE...]
where the time goes in v3:
time: 128 us
  Pallas kernels  125 us (98%)
  local copies, waits for them, and re-layouts  2.21 us (2%)
  between operations  1.29 us (1%)
    pallas_call x1, Pallas kernels, shards(): pl.pallas_call(kernel, out_shape=(jax.ShapeDtypeStruct((OWN * TAPS * GATE...  122 us

profile of v3, /device:TPU:1, one launch (start us, length us, event | category | flops | bytes accessed | tf_op | source)
XLA Modules:
  0.0 128.1 jit_solution(16430750587740395261)
XLA Ops:
  1.3 2.2 %reshape.23.refs_0_ = bf16[432,768]{1,0:T(8,128)(2,1)} reshape(bf16[12,9,4,768]{3,2,1,0:T(4,128)(2,1)} %bitcast.13) | data formatting | bytes 1327104 | tf_op jit(solution)/shard_map/reshape | solution.py:634
  3.5 122.3 %shard_map.165 = (bf16[432,768]{1,0:T(8,128)(2,1)}, f32[8,128]{1,0:T(8,128)}, bf16[216,384]{1,0:T(8,128)(2,1)}, f32[16,8,128]{2,1,0:T(8,128)}) custom-call(bf16[432,768]{1,0:T(8,128)(2,1)} %reshape.23.refs_0_, bf16[432,432]{1,0:T(8,128)(2,1)} %constant.14.clone.refs_1_, bf16[3,384,128]{2,1,0:T(8,128)(2,1)} %bitcast.14, ...), custom_call_target="tpu_custom_call" | custom-call | tf_op jit(solution)/shard_map/pallas_call | solution.py:641
  125.8 2.4 %shard_map.166 = (bf16[12,9,4,768]{3,2,1,0:T(4,128)(2,1)}, f32[4,12]{1,0:T(4,128)}, bf16[216,384]{1,0:T(8,128)(2,1)}, f32[16,2,384]{2,1,0:T(2,128)}) custom-call(bf16[432,768]{1,0:T(8,128)(2,1)} %get-tuple-element.12.wg, f32[8,128]{1,0:T(8,128)} %get-tuple-element.13.bg, bf16[216,384]{1,0:T(8,128)(2,1)} %get-tuple-element.14.hg, ...), custom_call_target="tpu_custom_call" | custom-call | tf_op jit(solution)/shard_map/pallas_call | solution.py:705

commit v4 on v3

--- a/solution.py
+++ b/solution.py
@@ -70,7 +70,7 @@
 
 (S_YX0, S_YX1, S_YX2, S_H1, S_H2, S_H3, S_YH1, S_YH2, S_COTH, S_COTZ, S_COTX, S_FR, S_FRC, S_HB1, S_HB2, S_HB1C, S_HB2C,
  S_DH3, S_DH2, S_DH1, S_HQ, S_HQC, S_ST, S_STL, S_DZN2, S_DZN1, S_DZ0, S_DZZ2, S_DZZ1, S_DZX2, S_DZX1, S_BI, S_WHZ, S_WHX, S_WF,
- S_PR, S_PT, S_PL, NSEM) = range(39)
+ S_WFA, S_WFB, S_PR, S_PT, S_PL, NSEM) = range(41)
 
 
 N_IN = 14
@@ -81,11 +81,11 @@
     held, refs = refs[:N_IN - 1], refs[N_IN - 1:]
     idx = inputs[N_IN - 1]
     (
-        wx, whp, whpt, yx, yh, rx, rh, hbuf, coth, cot4, cotz, cotb, fsend, fblk, hblk, dv_ref, dhp, dhr,
+        wt, whp, whpt, yx, yh, rx, rh, hbuf, coth, cot4, cotz, cotb, fsend, fblk, hblk, dv_ref, dhp, dhr,
         h8, hq, st_send, st_tile, stl_send, stl, dz_send, dznear, dzbuf, bi_send, bi, stack, scat,
         wsend, wrecv, xf, cc, vv, pbuf, psend, prec, psum, ptile, plead, film_col, film_q, flat, ssem, rsem, lsem,
     ) = refs
-    wsrc, a_ref, frames, e_ref, et_ref, bias, film, cot, hw, pack, rsel, unpack, spread = held
+    wsrc, a_ref, frames, bias, e_ref, et_ref, film, cot, hw, pack, rsel, unpack, spread = held
     li = lax.axis_index("lead")
     ti = lax.axis_index("tile")
 
@@ -162,13 +162,13 @@
     has_up = ti < T - 1
     has_down = ti > 0
 
-    for n in range(5):
+    for n in range(4):
         load(n).wait()
-    wt = nn(a_ref[...], wsrc[...]).astype(BF)
-    wx[...] = wt[:, :HID]
-    wth = wt[:, HID:]
-    whp[...] = nn(wth, e_ref[...]).astype(BF)
-    whpt[...] = nt(et_ref[...], wth).astype(BF)
+    outer = wsrc[...].astype(F32).reshape(OWN * TAPS * GATES, 2 * HID).astype(BF)
+    wt[...] = nn(a_ref[...], outer).astype(BF)
+    sub = lax.broadcasted_iota(jnp.int32, (OWN, OWN), 0)
+    lane = lax.broadcasted_iota(jnp.int32, (OWN, OWN), 1)
+    bias_cols = [jnp.sum(jnp.where(sub == lane, bias[j:j + 1, :], 0.0), axis=1, keepdims=True) for j in range(GATES)]
 
     def row_parts(g):
         parts = []
@@ -182,32 +182,14 @@
         return parts
 
     own_x = []
-    for t in range(3):
-        parts = row_parts(nn(wx[...], frames[t]))
+
+    def frame_parts(t):
+        parts = row_parts(nn(wt[:, 0:HID], frames[t]))
         for a in (0, 2):
             yx[t, a] = parts[a]
         own_x.append(parts[1])
-    for t in range(3):
-        fsend[:, 2 * t:2 * t + 2] = nn(et_ref[...], frames[t]).astype(BF).reshape(T, 2, PAD, W)
-    for n in range(5, N_IN - 1):
-        load(n).wait()
-    sub = lax.broadcasted_iota(jnp.int32, (OWN, OWN), 0)
-    lane = lax.broadcasted_iota(jnp.int32, (OWN, OWN), 1)
-    bias_cols = [jnp.sum(jnp.where(sub == lane, bias[j:j + 1, :], 0.0), axis=1, keepdims=True) for j in range(GATES)]
-    slot = lax.broadcasted_iota(jnp.int32, (16, 2, HID), 0)
-    lines = jnp.sum(jnp.where(slot == idx[0], film[...], 0.0), axis=0)
-    lines = jnp.concatenate([lines, jnp.zeros((6, HID), F32)], 0).T
-    film_col[...] = jnp.zeros_like(film_col)
-    for i in range(L):
-        film_col[i, 0:OWN, :] = lines[i * OWN:(i + 1) * OWN]
-    film_q[...] = lines.reshape(4, 96, 8)
-    for p in range(4):
-        cot4[p] = cot[96 * p:96 * (p + 1), :]
-    stack[...] = jnp.zeros_like(stack)
-    cc[...] = jnp.zeros_like(cc)
-    vv[...] = jnp.zeros_like(vv)
-    pbuf[...] = jnp.zeros_like(pbuf)
-
+
+    frame_parts(0)
     pl.semaphore_wait(bar, L + T - 2)
 
     def halo(src, dst, sem):
@@ -215,6 +197,10 @@
         send(src.at[2], dst.at[1], sem, tile_dev(down))
 
     halo(yx.at[0], rx.at[0], S_YX0)
+    for n in range(4, N_IN - 1):
+        load(n).wait()
+    whp[...] = nn(wt[:, HID:], e_ref[...]).astype(BF)
+    whpt[...] = nt(et_ref[...], wt[:, HID:]).astype(BF)
     def from_neighbours(r):
         return jnp.where(has_down, r[0], 0.0) + jnp.where(has_up, r[1], 0.0)
 
@@ -245,9 +231,29 @@
     state, h = cell(z, jnp.zeros((PAD, W), F32))
     saved.append(state)
     share_h(0, h)
-    halo(yx.at[1], rx.at[1], S_YX1)
-    halo(yx.at[2], rx.at[2], S_YX2)
+    for t in (1, 2):
+        frame_parts(t)
+        halo(yx.at[t], rx.at[t], (S_YX0, S_YX1, S_YX2)[t])
     send(cot, coth.at[0], S_COTH, tile_dev(lax.rem(ti + 2, T)))
+    for t in range(3):
+        fsend[:, 2 * t:2 * t + 2] = nn(et_ref[...], frames[t]).astype(BF).reshape(T, 2, PAD, W)
+    for p in range(4):
+        cot4[p] = cot[96 * p:96 * (p + 1), :]
+    slot = lax.broadcasted_iota(jnp.int32, (16, 2, HID), 0)
+    lines = jnp.sum(jnp.where(slot == idx[0], film[...], 0.0), axis=0)
+    lines = jnp.concatenate([lines, jnp.zeros((6, HID), F32)], 0).T
+    film_col[...] = jnp.zeros_like(film_col)
+    for i in range(L):
+        film_col[i, 0:OWN, :] = lines[i * OWN:(i + 1) * OWN]
+    film_q[...] = lines.reshape(4, 96, 8)
+    for at in (0, (T + 1) * W):
+        stack[:, at:at + W] = jnp.zeros((3 * GR, W), BF)
+    for at in (0, (T + 2) * W):
+        cc[:, at:at + 2 * W] = jnp.zeros((3 * 96, 2 * W), BF)
+    vv[96:W, :] = jnp.zeros((W - 96, T * W), BF)
+    for d in range(4):
+        pbuf[256 * d + 216:256 * (d + 1), :] = jnp.zeros((40, W), F32)
+    scat[...] = jnp.zeros_like(scat)
 
     def half(x):
         return x.at[pl.ds(3 * core, 3)]
@@ -400,25 +406,18 @@
         t = 2 - n
         src = dzbuf.at[n]
 
-        def body(row, carry):
-            block = src[row].astype(F32)
+        def body(r, carry):
+            block = src[r].astype(F32)
             for b in range(3):
-                piece = shifted(block, 1 - b).astype(BF)
-                for a in range(3):
-                    k = 3 * a + b
-                    at = pl.multiple_of((row + a) * W, W)
-                    stack[k * GR:(k + 1) * GR, pl.ds(at, W)] = piece
-            at = pl.multiple_of(row * W, W)
-            scat[0:2 * PAD, pl.ds(at, W)] = fblk[row, 2 * t:2 * t + 2].reshape(2 * PAD, W)
+                stack[b * GR:(b + 1) * GR, pl.ds(pl.multiple_of((r + 1) * W, W), W)] = shifted(block, 1 - b).astype(BF)
+            at = pl.multiple_of(r * W, W)
+            scat[0:2 * PAD, pl.ds(at, W)] = fblk[r, 2 * t:2 * t + 2].reshape(2 * PAD, W)
             if t > 0:
-                scat[2 * PAD:4 * PAD, pl.ds(at, W)] = hblk[t - 1, row].reshape(2 * PAD, W)
+                scat[2 * PAD:4 * PAD, pl.ds(at, W)] = hblk[t - 1, r].reshape(2 * PAD, W)
             return carry
 
-        lax.fori_loop(0, T, body, 0)
-        stack[0:3 * GR, T * W:(T + 1) * W] = jnp.zeros((3 * GR, W), BF)
-        stack[6 * GR:9 * GR, W:2 * W] = jnp.zeros((3 * GR, W), BF)
-        rows = 4 * PAD if t > 0 else 2 * PAD
-        return nt(scat[0:rows, :], stack[:, W:(T + 1) * W])
+        lax.fori_loop(0, T, body, 0, unroll=8)
+        return jnp.concatenate([nt(stack[:, (2 - a) * W:(2 - a + T) * W], scat[...]) for a in range(3)], 0).T
 
     def share_weights(n, x):
         y = nn((x * (1.0 / 256.0)).astype(BF), pack[...]).astype(BF)
@@ -429,7 +428,17 @@
         if n == 0:
             each_z(lambda to: send(src, dst.at[ti], S_WHZ, tile_dev(row * 4 + to)))
         else:
-            each_tile_far_first(lambda to: send(src, dst.at[ti], S_WF, tile_dev(to)))
+            send(src, dst.at[ti], S_WFA, tile_dev(row * 4 + lax.rem(col + 2, 4)))
+            for mx in (2, 1, 3, 0):
+                for mz in (1, 3, 0) if mx else (1, 3):
+                    to = lax.rem(row + mx, 4) * 4 + lax.rem(col + mz, 4)
+                    send(src, dst.at[ti], S_WF, tile_dev(to))
+
+    def forward_weights():
+        opposite = row * 4 + lax.rem(col + 2, 4)
+        got(wrecv.at[1, 0], S_WFA)
+        mine = wrecv.at[1, opposite]
+        each_x(lambda to: send(mine, mine, S_WFB, tile_dev(to * 4 + col)))
 
     def share_weights_x():
         got(wrecv.at[0, pl.ds(0, 3)], S_WHZ)
@@ -440,7 +449,8 @@
         if n == 0:
             got(wrecv.at[0, pl.ds(0, 12)], S_WHX)
         else:
-            got(wrecv.at[1, pl.ds(0, T - 1)], S_WF)
+            got(wrecv.at[1, pl.ds(0, 11)], S_WF)
+            got(wrecv.at[1, pl.ds(0, 3)], S_WFB)
         for s_ in range(T):
             block = wrecv[n, s_].astype(F32)
             xf[24 * s_:24 * (s_ + 1), 0:256] = block[0:24]
@@ -492,7 +502,7 @@
             for d in range(4):
                 pbuf[d * 256 + k * 24:d * 256 + (k + 1) * 24, :] = part[b * 96 + d * 24:b * 96 + (d + 1) * 24]
     psend[...] = pbuf[...].astype(BF).reshape(L, 32, W)
-    prec[li] = psend[li]
+    prec[li] = psend[8 * lax.rem(li, 4) + lax.div(li, 4)]
 
     dz, dc = gate_grads(1, await_dh(1), dc)
     bias_sum = bias_sum + dz
@@ -500,7 +510,7 @@
     back(1)
     share_dh(2)
     share_z(1)
-    each_lead(lambda to: send(psend.at[to], prec.at[li], S_PR, lead_dev(to)))
+    each_lead(lambda to: send(psend.at[8 * lax.rem(to, 4) + lax.div(to, 4)], prec.at[li], S_PR, lead_dev(to)))
     swap_blocks(1)
     swap_blocks(0)
     share_x(1)
@@ -510,6 +520,20 @@
     grads = weight_part(0)
 
     dz, dc = gate_grads(2, await_dh(2), dc)
+
+    got(prec.at[pl.ds(0, L - 1)], S_PR)
+    psum[...] = (jnp.sum(prec[...].astype(F32), axis=0) * (1.0 / 256.0)).astype(BF)
+    owner = col * 4 + lax.rem(li, 4)
+    gathers = lax.rem(li, 4) == col
+
+    @pl.when(owner != ti)
+    def _():
+        send(psum, ptile.at[row], S_PT, tile_dev(owner))
+
+    @pl.when(owner == ti)
+    def _():
+        ptile[row] = psum[...]
+
     await_x(1)
     await_blocks(0)
     grads = grads + weight_part(1)
@@ -523,24 +547,6 @@
     each_tile_far_first(lambda to: send(bi_send, bi.at[ti], S_BI, tile_dev(to)))
     bi[ti] = bi_send[...]
 
-    got(prec.at[pl.ds(0, L - 1)], S_PR)
-    psum[...] = (jnp.sum(prec[...].astype(F32), axis=0) * (1.0 / 256.0)).astype(BF)
-    owner = col * 4 + lax.div(li, 8)
-    gathers = lax.div(li, 8) == col
-
-    @pl.when(owner != ti)
-    def _():
-        send(psum, ptile.at[row], S_PT, tile_dev(owner))
-
-    @pl.when(owner == ti)
-    def _():
-        ptile[row] = psum[...]
-
-    got(dzbuf.at[2, pl.ds(0, T - 1)], S_DZ0)
-    grads0 = weight_part(2)
-    share_weights(1, grads[0:2 * PAD] + grads0)
-    share_weights_x()
-
     @pl.when(gathers)
     def _():
         @pl.when(owner == ti)
@@ -551,8 +557,14 @@
         def _():
             got(ptile, S_PT)
 
-        each_lead(lambda to: send(ptile, plead.at[lax.rem(li, 8)], S_PL, lead_dev(to)))
-        plead[lax.rem(li, 8)] = ptile[...]
+        each_lead(lambda to: send(ptile, plead.at[lax.div(li, 4)], S_PL, lead_dev(to)))
+        plead[lax.div(li, 4)] = ptile[...]
+
+    got(dzbuf.at[2, pl.ds(0, T - 1)], S_DZ0)
+    share_weights_x()
+    grads0 = weight_part(2)
+    share_weights(1, grads[0:2 * PAD] + grads0[0:2 * PAD])
+    forward_weights()
 
     got(stl.at[pl.ds(0, L - 1)], S_STL)
 
@@ -593,7 +605,9 @@
     sent(dzbuf.at[2, pl.ds(0, T - 1)], S_DZ0)
     sent(wrecv.at[0, pl.ds(0, 3)], S_WHZ)
     sent(wrecv.at[0, pl.ds(0, 12)], S_WHX)
-    sent(wrecv.at[1, pl.ds(0, T - 1)], S_WF)
+    sent(wrecv.at[1, pl.ds(0, 11)], S_WF)
+    sent(wrecv.at[1, 0], S_WFA)
+    sent(wrecv.at[1, pl.ds(0, 3)], S_WFB)
     sent(coth, S_COTH)
     sent(cotz.at[pl.ds(0, 3)], S_COTZ)
     sent(cotb.at[pl.ds(0, 12)], S_COTX)
@@ -631,11 +645,11 @@
 
 def shards(frames, enc_weight, enc_bias, head_weight, film_table, lead_index, cotangent):
     a, pack, unpack, e, et, spread, rsel = [jnp.asarray(x) for x in one_hots()]
-    wsrc = enc_weight.transpose(0, 2, 1, 3).reshape(OWN * TAPS * GATES, 2 * HID)
+    wsrc = enc_weight.transpose(0, 2, 1, 3)
     hw = head_weight.transpose(1, 0, 2).reshape(TAPS * HID, HID)
     vm = pltpu.VMEM
     inputs = (
-        wsrc, a, frames.reshape(3, HID, W), e, et, enc_bias.T, film_table, cotangent.reshape(HID, W), hw, pack, rsel,
+        wsrc, a, frames.reshape(3, HID, W), enc_bias.T, e, et, film_table, cotangent.reshape(HID, W), hw, pack, rsel,
         unpack, spread,
     )
     outs = pl.pallas_call(
@@ -649,7 +663,7 @@
         in_specs=[pl.BlockSpec(memory_space=pl.ANY)] * (N_IN - 1) + [pl.BlockSpec(memory_space=pltpu.SMEM)],
         out_specs=(pl.BlockSpec(memory_space=vm),) * 4,
         scratch_shapes=[vm(x.shape, x.dtype) for x in inputs] + [
-            vm((TAPS * GR, HID), BF),
+            vm((TAPS * GR, 2 * HID), BF),
             vm((TAPS * GR, CP), BF),
             vm((CP, TAPS * GR), BF),
             vm((3, 3, GR, W), F32),
@@ -678,7 +692,7 @@
             vm((3, T, GR, W), BF),
             vm((8, W), F32),
             vm((T, 8, W), F32),
-            vm((TAPS * GR, (T + 2) * W), BF),
+            vm((3 * GR, (T + 2) * W), BF),
             vm((4 * PAD, T * W), BF),
             vm((2, 48, 256), BF),
             vm((2, T, 48, 256), BF),

time: 128 us -> 115 us (0.90); the launches traced: 128 us -> 113 us
  Pallas kernels: 125 us -> 112 us
  local copies, waits for them, and re-layouts: 2.21 us -> 0 us
    pallas_call x1, Pallas kernels: 122 us -> 110 us  [shards(): pl.pallas_call(kernel, out_shape=(jax.ShapeDtypeStruct((OWN * TAPS * GATE...]
    reshape x1 -> x0, local copies, waits for them, and re-layouts: 2.21 us -> none  [shards(): wsrc = enc_weight.transpose(0, 2, 1, 3).reshape(OWN * TAPS * GATES, 2 * HID)]
where the time goes in v4:
time: 115 us; the launch traced here: 113 us
  Pallas kernels  112 us (97%)
  between operations  1.29 us (1%)
    pallas_call x1, Pallas kernels, shards(): pl.pallas_call(kernel, out_shape=(jax.ShapeDtypeStruct((OWN * TAPS * GATE...  110 us
    pallas_call x1, Pallas kernels, shards(): pl.pallas_call(finish, out_shape=(jax.ShapeDtypeStruct((OWN, TAPS, GATES,...  2.36 us

profile of v4, /device:TPU:1, one launch (start us, length us, event | category | flops | bytes accessed | tf_op | source)
XLA Modules:
  0.0 113.2 jit_solution(18296820840310272870)
XLA Ops:
  1.3 109.5 %shard_map.165 = (bf16[432,768]{1,0:T(8,128)(2,1)}, f32[8,128]{1,0:T(8,128)}, bf16[216,384]{1,0:T(8,128)(2,1)}, f32[16,8,128]{2,1,0:T(8,128)}) custom-call(bf16[12,9,4,768]{3,2,1,0:T(4,128)(2,1)} %bitcast.13, bf16[432,432]{1,0:T(8,128)(2,1)} %constant.14.clone.refs_1_, bf16[3,384,128]{2,1,0:T(8,128)(2,1)} %bitcast.14, f32[4,12]{1,0:T(4,128)} %bitcast.16, ...), custom_call_target="tpu_custom_call" | custom-call | tf_op jit(solution)/shard_map/pallas_call | solution.py:655
  110.8 2.4 %shard_map.166 = (bf16[12,9,4,768]{3,2,1,0:T(4,128)(2,1)}, f32[4,12]{1,0:T(4,128)}, bf16[216,384]{1,0:T(8,128)(2,1)}, f32[16,2,384]{2,1,0:T(2,128)}) custom-call(bf16[432,768]{1,0:T(8,128)(2,1)} %get-tuple-element.12.wg, f32[8,128]{1,0:T(8,128)} %get-tuple-element.13.bg, bf16[216,384]{1,0:T(8,128)(2,1)} %get-tuple-element.14.hg, ...), custom_call_target="tpu_custom_call" | custom-call | tf_op jit(solution)/shard_map/pallas_call | solution.py:719

commit v5 on v4

--- a/solution.py
+++ b/solution.py
@@ -70,7 +70,7 @@
 
 (S_YX0, S_YX1, S_YX2, S_H1, S_H2, S_H3, S_YH1, S_YH2, S_COTH, S_COTZ, S_COTX, S_FR, S_FRC, S_HB1, S_HB2, S_HB1C, S_HB2C,
  S_DH3, S_DH2, S_DH1, S_HQ, S_HQC, S_ST, S_STL, S_DZN2, S_DZN1, S_DZ0, S_DZZ2, S_DZZ1, S_DZX2, S_DZX1, S_BI, S_WHZ, S_WHX, S_WF,
- S_WFA, S_WFB, S_PR, S_PT, S_PL, NSEM) = range(41)
+ S_WFA, S_WFB, S_PR, S_PT, S_PL, S_COTH2, NSEM) = range(42)
 
 
 N_IN = 14
@@ -81,7 +81,7 @@
     held, refs = refs[:N_IN - 1], refs[N_IN - 1:]
     idx = inputs[N_IN - 1]
     (
-        wt, whp, whpt, yx, yh, rx, rh, hbuf, coth, cot4, cotz, cotb, fsend, fblk, hblk, dv_ref, dhp, dhr,
+        wt, whp, whpt, whpt2, dvt_ref, yx, yh, rx, rh, hbuf, coth, cot4, cotz, cotb, fsend, fblk, hblk, dv_ref, dhp, dhr,
         h8, hq, st_send, st_tile, stl_send, stl, dz_send, dznear, dzbuf, bi_send, bi, stack, scat,
         wsend, wrecv, xf, cc, vv, pbuf, psend, prec, psum, ptile, plead, film_col, film_q, flat, ssem, rsem, lsem,
     ) = refs
@@ -170,24 +170,18 @@
     lane = lax.broadcasted_iota(jnp.int32, (OWN, OWN), 1)
     bias_cols = [jnp.sum(jnp.where(sub == lane, bias[j:j + 1, :], 0.0), axis=1, keepdims=True) for j in range(GATES)]
 
-    def row_parts(g):
-        parts = []
-        for a in range(3):
-            total = None
-            for b in range(3):
-                k = 3 * a + b
-                term = shifted(g[k * GR:(k + 1) * GR], b - 1)
-                total = term if total is None else total + term
-            parts.append(total)
-        return parts
+    def row_part(g):
+        return sum(shifted(g[b * GR:(b + 1) * GR], b - 1) for b in range(3))
+
+    def tap_rows(a):
+        return slice(3 * a * GR, 3 * (a + 1) * GR)
 
     own_x = []
 
     def frame_parts(t):
-        parts = row_parts(nn(wt[:, 0:HID], frames[t]))
         for a in (0, 2):
-            yx[t, a] = parts[a]
-        own_x.append(parts[1])
+            yx[t, a] = row_part(nn(wt[tap_rows(a), 0:HID], frames[t]))
+        own_x.append(None if t == 0 else row_part(nn(wt[tap_rows(1), 0:HID], frames[t])))
 
     frame_parts(0)
     pl.semaphore_wait(bar, L + T - 2)
@@ -197,10 +191,12 @@
         send(src.at[2], dst.at[1], sem, tile_dev(down))
 
     halo(yx.at[0], rx.at[0], S_YX0)
+    own_x[0] = row_part(nn(wt[tap_rows(1), 0:HID], frames[0]))
     for n in range(4, N_IN - 1):
         load(n).wait()
     whp[...] = nn(wt[:, HID:], e_ref[...]).astype(BF)
-    whpt[...] = nt(et_ref[...], wt[:, HID:]).astype(BF)
+    whpt[...] = nt(et_ref[...], wt[tap_rows(1), HID:]).astype(BF)
+    whpt2[...] = nt(et_ref[...], jnp.concatenate([wt[tap_rows(0), HID:], wt[tap_rows(2), HID:]], 0)).astype(BF)
     def from_neighbours(r):
         return jnp.where(has_down, r[0], 0.0) + jnp.where(has_up, r[1], 0.0)
 
@@ -261,40 +257,53 @@
     def send_frames(to):
         send(half(fsend.at[to]), half(fblk.at[ti]), S_FR, tile_dev(to))
 
+    zero_row = jnp.zeros((HID, W), BF)
+
+    def head_product(a, x):
+        ct = x.astype(F32).T
+        total = None
+        for b in range(3):
+            k = 3 * a + b
+            term = nn(shifted_rows(ct, -2 * (b - 1)).astype(BF), hw[k * HID:(k + 1) * HID, :])
+            total = term if total is None else total + term
+        return total
+
     for t in (1, 2):
         await_h(t - 1)
-        parts = row_parts(nn(whp[...], hbuf[t - 1].reshape(CP, W)))
+        h = hbuf[t - 1].reshape(CP, W)
         for a in (0, 2):
-            yh[t - 1, a] = parts[a]
+            yh[t - 1, a] = row_part(nn(whp[tap_rows(a), :], h))
         sem = (S_YH1, S_YH2)[t - 1]
         halo(yh.at[t - 1], rh.at[t - 1], sem)
         got(rx.at[t], (S_YX0, S_YX1, S_YX2)[t])
-        base = own_x[t] + from_neighbours(rx.at[t]) + parts[1]
+        base = own_x[t] + from_neighbours(rx.at[t]) + row_part(nn(whp[tap_rows(1), :], h))
         got(rh.at[t - 1], sem)
         z = base + from_neighbours(rh.at[t - 1])
         state, h = cell(z, saved[-1][5])
         saved.append(state)
         share_h(t, h)
         if t == 1:
-            send(cot, coth.at[1], S_COTH, tile_dev(lax.rem(ti + T - 2, T)))
+            send(cot, coth.at[1], S_COTH2, tile_dev(lax.rem(ti + T - 2, T)))
+            dvt = head_product(1, cot[...])
+            got(coth.at[0], S_COTH)
+            dvt_ref[...] = dvt + head_product(2, jnp.where(ti >= 2, coth[0], zero_row))
     each_tile_far_first(send_frames)
     fblk[ti, pl.ds(3 * core, 3)] = fsend[ti, pl.ds(3 * core, 3)]
     each_z(lambda to: send(cot4.at[to], cotz.at[col], S_COTZ, tile_dev(row * 4 + to)))
     cotz[col] = cot4[col]
-    got(coth, S_COTH)
-    zero = jnp.zeros((HID, W), BF)
-    rows = (jnp.where(ti < T - 2, coth[1], zero), cot[...], jnp.where(ti >= 2, coth[0], zero))
-    dvt = jnp.zeros((W, HID), F32)
-    for a in range(3):
-        ct = rows[a].astype(F32).T
-        for b in range(3):
-            k = 3 * a + b
-            dvt = dvt + nn(shifted_rows(ct, -2 * (b - 1)).astype(BF), hw[k * HID:(k + 1) * HID, :])
-    dv = dvt.T
+    got(coth.at[1], S_COTH2)
+    dv = (dvt_ref[...] + head_product(0, jnp.where(ti < T - 2, coth[1], zero_row))).T
     dv_ref[...] = jnp.zeros_like(dv_ref)
     for i in range(L):
         dv_ref[0, i, 0:OWN, :] = dv[i * OWN:(i + 1) * OWN]
     dv_ref[1] = nn(et_ref[...], cot[...]).reshape(L, PAD, W)
+    factors = []
+    for i_g, f_g, g_g, o_g, previous, now in saved:
+        sq = jnp.tanh(now)
+        factors.append((
+            o_g * (1.0 - sq * sq), g_g * i_g * (1.0 - i_g), previous * f_g * (1.0 - f_g), i_g * (1.0 - g_g * g_g),
+            sq * o_g * (1.0 - o_g), f_g,
+        ))
 
     def share_blocks(t):
         hsem = (S_HB1, S_HB2)[t]
@@ -355,18 +364,9 @@
     dc = jnp.zeros((PAD, W), F32)
 
     def gate_grads(n, dh, dc):
-        i_g, f_g, g_g, o_g, previous, now = saved[2 - n]
-        sq = jnp.tanh(now)
-        dc = dc + dh * o_g * (1.0 - sq * sq)
-        dz = jnp.concatenate(
-            [x[0:OWN] for x in (
-                dc * g_g * i_g * (1.0 - i_g),
-                dc * previous * f_g * (1.0 - f_g),
-                dc * i_g * (1.0 - g_g * g_g),
-                dh * sq * o_g * (1.0 - o_g),
-            )],
-            0,
-        )
+        to_c, to_i, to_f, to_g, to_o, f_g = factors[2 - n]
+        dc = dc + dh * to_c
+        dz = jnp.concatenate([x[0:OWN] for x in (dc * to_i, dc * to_f, dc * to_g, dh * to_o)], 0)
         src = dz_send.at[n]
         dst = dzbuf.at[n]
         src[...] = dz.astype(BF)
@@ -394,13 +394,16 @@
 
     def back(n):
         zero = jnp.zeros((GR, W), F32)
-        rows = (
-            jnp.where(has_up, dznear[n, 1].astype(F32), zero),
-            dz_send[n].astype(F32),
-            jnp.where(has_down, dznear[n, 0].astype(F32), zero),
-        )
-        pieces = [shifted(rows[a], 1 - b).astype(BF) for a in range(3) for b in range(3)]
-        dhp[n + 1] = nn(whpt[...], jnp.concatenate(pieces, 0)).astype(BF).reshape(L, PAD, W)
+
+        def stacked(x):
+            return [shifted(x, 1 - b).astype(BF) for b in range(3)]
+
+        own = nn(whpt[...], jnp.concatenate(stacked(dz_send[n].astype(F32)), 0))
+        await_near(n)
+        above = stacked(jnp.where(has_up, dznear[n, 1].astype(F32), zero))
+        below = stacked(jnp.where(has_down, dznear[n, 0].astype(F32), zero))
+        whole = own + nn(whpt2[...], jnp.concatenate(above + below, 0))
+        dhp[n + 1] = whole.astype(BF).reshape(L, PAD, W)
 
     def weight_part(n):
         t = 2 - n
@@ -461,7 +464,6 @@
 
     dz, dc = gate_grads(0, await_dh(0), dc)
     bias_sum = bias_sum + dz
-    await_near(0)
     back(0)
     share_dh(1)
     share_z(0)
@@ -506,7 +508,6 @@
 
     dz, dc = gate_grads(1, await_dh(1), dc)
     bias_sum = bias_sum + dz
-    await_near(1)
     back(1)
     share_dh(2)
     share_z(1)
@@ -608,7 +609,8 @@
     sent(wrecv.at[1, pl.ds(0, 11)], S_WF)
     sent(wrecv.at[1, 0], S_WFA)
     sent(wrecv.at[1, pl.ds(0, 3)], S_WFB)
-    sent(coth, S_COTH)
+    sent(coth.at[0], S_COTH)
+    sent(coth.at[1], S_COTH2)
     sent(cotz.at[pl.ds(0, 3)], S_COTZ)
     sent(cotb.at[pl.ds(0, 12)], S_COTX)
     sent(fblk.at[pl.ds(0, T - 1), pl.ds(0, 3)], S_FR)
@@ -665,7 +667,9 @@
         scratch_shapes=[vm(x.shape, x.dtype) for x in inputs] + [
             vm((TAPS * GR, 2 * HID), BF),
             vm((TAPS * GR, CP), BF),
-            vm((CP, TAPS * GR), BF),
+            vm((CP, 3 * GR), BF),
+            vm((CP, 6 * GR), BF),
+            vm((W, HID), F32),
             vm((3, 3, GR, W), F32),
             vm((2, 3, GR, W), F32),
             vm((3, 2, GR, W), F32),

time: 115 us -> 115 us (level)
  no operation moved by 1% of the time
where the time goes in v5:
time: 115 us; the launch traced here: 113 us
  Pallas kernels  112 us (97%)
  between operations  1.29 us (1%)
    pallas_call x1, Pallas kernels, shards(): pl.pallas_call(kernel, out_shape=(jax.ShapeDtypeStruct((OWN * TAPS * GATE...  109 us
    pallas_call x1, Pallas kernels, shards(): pl.pallas_call(finish, out_shape=(jax.ShapeDtypeStruct((OWN, TAPS, GATES,...  2.36 us

profile of v5, /device:TPU:1, one launch (start us, length us, event | category | flops | bytes accessed | tf_op | source)
XLA Modules:
  0.0 113.1 jit_solution(17904278636136314024)
XLA Ops:
  1.3 109.4 %shard_map.165 = (bf16[432,768]{1,0:T(8,128)(2,1)}, f32[8,128]{1,0:T(8,128)}, bf16[216,384]{1,0:T(8,128)(2,1)}, f32[16,8,128]{2,1,0:T(8,128)}) custom-call(bf16[12,9,4,768]{3,2,1,0:T(4,128)(2,1)} %bitcast.13, bf16[432,432]{1,0:T(8,128)(2,1)} %constant.14.clone.refs_1_, bf16[3,384,128]{2,1,0:T(8,128)(2,1)} %bitcast.14, f32[4,12]{1,0:T(4,128)} %bitcast.16, ...), custom_call_target="tpu_custom_call" | custom-call | tf_op jit(solution)/shard_map/pallas_call | solution.py:657
  110.7 2.4 %shard_map.166 = (bf16[12,9,4,768]{3,2,1,0:T(4,128)(2,1)}, f32[4,12]{1,0:T(4,128)}, bf16[216,384]{1,0:T(8,128)(2,1)}, f32[16,2,384]{2,1,0:T(2,128)}) custom-call(bf16[432,768]{1,0:T(8,128)(2,1)} %get-tuple-element.12.wg, f32[8,128]{1,0:T(8,128)} %get-tuple-element.13.bg, bf16[216,384]{1,0:T(8,128)(2,1)} %get-tuple-element.14.hg, ...), custom_call_target="tpu_custom_call" | custom-call | tf_op jit(solution)/shard_map/pallas_call | solution.py:723

commit v6 on v5

--- a/solution.py
+++ b/solution.py
@@ -81,7 +81,7 @@
     held, refs = refs[:N_IN - 1], refs[N_IN - 1:]
     idx = inputs[N_IN - 1]
     (
-        wt, whp, whpt, whpt2, dvt_ref, yx, yh, rx, rh, hbuf, coth, cot4, cotz, cotb, fsend, fblk, hblk, dv_ref, dhp, dhr,
+        wt, whp, whpt, dvt_ref, yx, yh, rx, rh, hbuf, coth, cot4, cotz, cotb, fsend, fblk, hblk, dv_ref, dhp, dhr,
         h8, hq, st_send, st_tile, stl_send, stl, dz_send, dznear, dzbuf, bi_send, bi, stack, scat,
         wsend, wrecv, xf, cc, vv, pbuf, psend, prec, psum, ptile, plead, film_col, film_q, flat, ssem, rsem, lsem,
     ) = refs
@@ -170,18 +170,16 @@
     lane = lax.broadcasted_iota(jnp.int32, (OWN, OWN), 1)
     bias_cols = [jnp.sum(jnp.where(sub == lane, bias[j:j + 1, :], 0.0), axis=1, keepdims=True) for j in range(GATES)]
 
-    def row_part(g):
-        return sum(shifted(g[b * GR:(b + 1) * GR], b - 1) for b in range(3))
-
-    def tap_rows(a):
-        return slice(3 * a * GR, 3 * (a + 1) * GR)
+    def row_parts(g):
+        return [sum(shifted(g[(3 * a + b) * GR:(3 * a + b + 1) * GR], b - 1) for b in range(3)) for a in range(3)]
 
     own_x = []
 
     def frame_parts(t):
+        parts = row_parts(nn(wt[:, 0:HID], frames[t]))
         for a in (0, 2):
-            yx[t, a] = row_part(nn(wt[tap_rows(a), 0:HID], frames[t]))
-        own_x.append(None if t == 0 else row_part(nn(wt[tap_rows(1), 0:HID], frames[t])))
+            yx[t, a] = parts[a].astype(BF)
+        own_x.append(parts[1])
 
     frame_parts(0)
     pl.semaphore_wait(bar, L + T - 2)
@@ -191,14 +189,12 @@
         send(src.at[2], dst.at[1], sem, tile_dev(down))
 
     halo(yx.at[0], rx.at[0], S_YX0)
-    own_x[0] = row_part(nn(wt[tap_rows(1), 0:HID], frames[0]))
     for n in range(4, N_IN - 1):
         load(n).wait()
     whp[...] = nn(wt[:, HID:], e_ref[...]).astype(BF)
-    whpt[...] = nt(et_ref[...], wt[tap_rows(1), HID:]).astype(BF)
-    whpt2[...] = nt(et_ref[...], jnp.concatenate([wt[tap_rows(0), HID:], wt[tap_rows(2), HID:]], 0)).astype(BF)
+    whpt[...] = nt(et_ref[...], wt[:, HID:]).astype(BF)
     def from_neighbours(r):
-        return jnp.where(has_down, r[0], 0.0) + jnp.where(has_up, r[1], 0.0)
+        return jnp.where(has_down, r[0].astype(F32), 0.0) + jnp.where(has_up, r[1].astype(F32), 0.0)
 
     def padded(x):
         return jnp.concatenate([x, jnp.zeros((PAD - OWN, W), F32)], 0)
@@ -270,13 +266,13 @@
 
     for t in (1, 2):
         await_h(t - 1)
-        h = hbuf[t - 1].reshape(CP, W)
+        parts = row_parts(nn(whp[...], hbuf[t - 1].reshape(CP, W)))
         for a in (0, 2):
-            yh[t - 1, a] = row_part(nn(whp[tap_rows(a), :], h))
+            yh[t - 1, a] = parts[a].astype(BF)
         sem = (S_YH1, S_YH2)[t - 1]
         halo(yh.at[t - 1], rh.at[t - 1], sem)
         got(rx.at[t], (S_YX0, S_YX1, S_YX2)[t])
-        base = own_x[t] + from_neighbours(rx.at[t]) + row_part(nn(whp[tap_rows(1), :], h))
+        base = own_x[t] + from_neighbours(rx.at[t]) + parts[1]
         got(rh.at[t - 1], sem)
         z = base + from_neighbours(rh.at[t - 1])
         state, h = cell(z, saved[-1][5])
@@ -398,11 +394,10 @@
         def stacked(x):
             return [shifted(x, 1 - b).astype(BF) for b in range(3)]
 
-        own = nn(whpt[...], jnp.concatenate(stacked(dz_send[n].astype(F32)), 0))
         await_near(n)
         above = stacked(jnp.where(has_up, dznear[n, 1].astype(F32), zero))
         below = stacked(jnp.where(has_down, dznear[n, 0].astype(F32), zero))
-        whole = own + nn(whpt2[...], jnp.concatenate(above + below, 0))
+        whole = nn(whpt[...], jnp.concatenate(above + stacked(dz_send[n].astype(F32)) + below, 0))
         dhp[n + 1] = whole.astype(BF).reshape(L, PAD, W)
 
     def weight_part(n):
@@ -458,9 +453,9 @@
             block = wrecv[n, s_].astype(F32)
             xf[24 * s_:24 * (s_ + 1), 0:256] = block[0:24]
             xf[24 * s_:24 * (s_ + 1), 256:512] = block[24:48]
-        out = nt(unpack[...], xf[...].astype(BF)).astype(BF)
-        col = HID * (1 - n)
-        wg_out[:, col:col + HID] = out
+        out = nt(unpack[...], xf[...].astype(BF)).reshape(OWN, TAPS, GATES, HID).astype(BF)
+        first = HID * (1 - n)
+        wg_out[:, :, :, first:first + HID] = out
 
     dz, dc = gate_grads(0, await_dh(0), dc)
     bias_sum = bias_sum + dz
@@ -575,9 +570,14 @@
 
     acc = lax.fori_loop(0, L, table, tuple(jnp.zeros((8, W), F32) for _ in range(16)))
     for m in range(16):
-        fg_out[m] = acc[m] * (1.0 / 256.0)
+        rows6 = acc[m] * (1.0 / 256.0)
+        for n in range(2):
+            for q in range(3):
+                fg_out[m, n:n + 1, W * q:W * (q + 1)] = rows6[3 * n + q:3 * n + q + 1]
     got(bi.at[pl.ds(0, T - 1)], S_BI)
-    bg_out[...] = jnp.sum(bi[...], axis=0) * (1.0 / 256.0)
+    line = jnp.sum(bi[...], axis=0) * (1.0 / 256.0)
+    for j in range(GATES):
+        bg_out[j:j + 1, :] = line[0:1, j * OWN:(j + 1) * OWN]
     finish_weights(0)
 
     @pl.when(gathers)
@@ -634,15 +634,14 @@
         lax.fori_loop(1, L, body, 0)
 
 
-def finish(wg, bg, hg, fg, wg_out, bg_out, hg_out, fg_out):
-    wg_out[...] = wg[...].astype(F32).reshape(OWN, TAPS, GATES, 2 * HID).astype(BF)
-    hg_out[...] = hg[...]
-    for j in range(GATES):
-        bg_out[j:j + 1, :] = bg[0:1, j * OWN:(j + 1) * OWN]
-    for m in range(16):
-        for n in range(2):
-            for q in range(3):
-                fg_out[m, n:n + 1, W * q:W * (q + 1)] = fg[m, 3 * n + q:3 * n + q + 1, :]
+def finish(*refs):
+    sems = refs[8]
+    copies = [pltpu.make_async_copy(refs[0].at[n], refs[4].at[n], sems.at[n]) for n in range(OWN)]
+    copies += [pltpu.make_async_copy(refs[n], refs[n + 4], sems.at[OWN + n]) for n in (1, 2, 3)]
+    for copy in copies:
+        copy.start()
+    for copy in copies:
+        copy.wait()
 
 
 def shards(frames, enc_weight, enc_bias, head_weight, film_table, lead_index, cotangent):
@@ -657,23 +656,22 @@
     outs = pl.pallas_call(
         kernel,
         out_shape=(
-            jax.ShapeDtypeStruct((OWN * TAPS * GATES, 2 * HID), BF),
-            jax.ShapeDtypeStruct((8, W), F32),
+            jax.ShapeDtypeStruct((OWN, TAPS, GATES, 2 * HID), BF),
+            jax.ShapeDtypeStruct((GATES, OWN), F32),
             jax.ShapeDtypeStruct((TAPS * 24, HID), BF),
-            jax.ShapeDtypeStruct((16, 8, W), F32),
+            jax.ShapeDtypeStruct((16, 2, HID), F32),
         ),
         in_specs=[pl.BlockSpec(memory_space=pl.ANY)] * (N_IN - 1) + [pl.BlockSpec(memory_space=pltpu.SMEM)],
         out_specs=(pl.BlockSpec(memory_space=vm),) * 4,
         scratch_shapes=[vm(x.shape, x.dtype) for x in inputs] + [
             vm((TAPS * GR, 2 * HID), BF),
             vm((TAPS * GR, CP), BF),
-            vm((CP, 3 * GR), BF),
-            vm((CP, 6 * GR), BF),
+            vm((CP, TAPS * GR), BF),
             vm((W, HID), F32),
-            vm((3, 3, GR, W), F32),
-            vm((2, 3, GR, W), F32),
-            vm((3, 2, GR, W), F32),
-            vm((2, 2, GR, W), F32),
+            vm((3, 3, GR, W), BF),
+            vm((2, 3, GR, W), BF),
+            vm((3, 2, GR, W), BF),
+            vm((2, 2, GR, W), BF),
             vm((3, L, PAD, W), BF),
             vm((2, HID, W), BF),
             vm((4, 96, W), BF),
@@ -728,8 +726,9 @@
             jax.ShapeDtypeStruct((TAPS * 24, HID), BF),
             jax.ShapeDtypeStruct((16, 2, HID), F32),
         ),
-        in_specs=[pl.BlockSpec(memory_space=vm)] * 4,
-        out_specs=(pl.BlockSpec(memory_space=vm),) * 4,
+        in_specs=[pl.BlockSpec(memory_space=pl.ANY)] * 4,
+        out_specs=(pl.BlockSpec(memory_space=pl.ANY),) * 4,
+        scratch_shapes=[pltpu.SemaphoreType.DMA((OWN + 4,))],
     )(*outs)
     return wg.transpose(0, 2, 1, 3), bg.T, hg.reshape(TAPS, 24, HID).transpose(1, 0, 2), fg
 

time: 115 us -> 139 us (1.21)
  Pallas kernels: 112 us -> 136 us
    pallas_call x1, Pallas kernels: 2.36 us -> 27.9 us  [shards(): pl.pallas_call(finish, out_shape=(jax.ShapeDtypeStruct((OWN, TAPS, GATES,...]
where the time goes in v6:
time: 139 us; the launch traced here: 138 us
  Pallas kernels  136 us (98%)
    pallas_call x1, Pallas kernels, shards(): pl.pallas_call(kernel, out_shape=(jax.ShapeDtypeStruct((OWN, TAPS, GATES,...  108 us
    pallas_call x1, Pallas kernels, shards(): pl.pallas_call(finish, out_shape=(jax.ShapeDtypeStruct((OWN, TAPS, GATES,...  27.9 us

profile of v6, /device:TPU:1, one launch (start us, length us, event | category | flops | bytes accessed | tf_op | source)
XLA Modules:
  0.0 137.5 jit_solution(5027317043023348118)
XLA Ops:
  1.3 108.3 %shard_map.165 = (bf16[12,9,4,768]{3,2,1,0:T(4,128)(2,1)}, f32[4,12]{1,0:T(4,128)}, bf16[216,384]{1,0:T(8,128)(2,1)}, f32[16,2,384]{2,1,0:T(2,128)}) custom-call(bf16[12,9,4,768]{3,2,1,0:T(4,128)(2,1)} %bitcast.13, bf16[432,432]{1,0:T(8,128)(2,1)} %constant.14.clone.refs_1_, bf16[3,384,128]{2,1,0:T(8,128)(2,1)} %bitcast.14, f32[4,12]{1,0:T(4,128)} %bitcast.16, ...), custom_call_target="tpu_custom_call" | custom-call | tf_op jit(solution)/shard_map/pallas_call | solution.py:656
  109.6 27.9 %shard_map.166 = (bf16[12,9,4,768]{3,2,1,0:T(4,128)(2,1)}, f32[4,12]{1,0:T(4,128)}, bf16[216,384]{1,0:T(8,128)(2,1)}, f32[16,2,384]{2,1,0:T(2,128)}) custom-call(bf16[12,9,4,768]{3,2,1,0:T(4,128)(2,1)} %get-tuple-element.12.refs_0_, f32[4,12]{1,0:T(4,128)} %get-tuple-element.13.refs_1_, bf16[216,384]{1,0:T(8,128)(2,1)} %get-tuple-element.14.refs_2_, ...), custom_call_target="tpu_custom_call" | custom-call | tf_op jit(solution)/shard_map/pallas_call | solution.py:721

commit v7 on v6

--- a/solution.py
+++ b/solution.py
@@ -453,9 +453,8 @@
             block = wrecv[n, s_].astype(F32)
             xf[24 * s_:24 * (s_ + 1), 0:256] = block[0:24]
             xf[24 * s_:24 * (s_ + 1), 256:512] = block[24:48]
-        out = nt(unpack[...], xf[...].astype(BF)).reshape(OWN, TAPS, GATES, HID).astype(BF)
         first = HID * (1 - n)
-        wg_out[:, :, :, first:first + HID] = out
+        wg_out[:, first:first + HID] = nt(unpack[...], xf[...].astype(BF)).astype(BF)
 
     dz, dc = gate_grads(0, await_dh(0), dc)
     bias_sum = bias_sum + dz
@@ -634,14 +633,11 @@
         lax.fori_loop(1, L, body, 0)
 
 
-def finish(*refs):
-    sems = refs[8]
-    copies = [pltpu.make_async_copy(refs[0].at[n], refs[4].at[n], sems.at[n]) for n in range(OWN)]
-    copies += [pltpu.make_async_copy(refs[n], refs[n + 4], sems.at[OWN + n]) for n in (1, 2, 3)]
-    for copy in copies:
-        copy.start()
-    for copy in copies:
-        copy.wait()
+def finish(wg, bg, hg, fg, wg_out, bg_out, hg_out, fg_out):
+    wg_out[...] = wg[...].astype(F32).reshape(OWN, TAPS, GATES, 2 * HID).astype(BF)
+    bg_out[...] = bg[...]
+    hg_out[...] = hg[...]
+    fg_out[...] = fg[...]
 
 
 def shards(frames, enc_weight, enc_bias, head_weight, film_table, lead_index, cotangent):
@@ -656,7 +652,7 @@
     outs = pl.pallas_call(
         kernel,
         out_shape=(
-            jax.ShapeDtypeStruct((OWN, TAPS, GATES, 2 * HID), BF),
+            jax.ShapeDtypeStruct((OWN * TAPS * GATES, 2 * HID), BF),
             jax.ShapeDtypeStruct((GATES, OWN), F32),
             jax.ShapeDtypeStruct((TAPS * 24, HID), BF),
             jax.ShapeDtypeStruct((16, 2, HID), F32),
@@ -715,7 +711,7 @@
             pltpu.SemaphoreType.DMA((N_IN - 1,)),
         ],
         compiler_params=pltpu.CompilerParams(
-            collective_id=0, has_side_effects=True, vmem_limit_bytes=56 * 2**20
+            collective_id=0, has_side_effects=True, vmem_limit_bytes=24 * 2**20
         ),
     )(*inputs, lead_index)
     wg, bg, hg, fg = pl.pallas_call(
@@ -726,9 +722,8 @@
             jax.ShapeDtypeStruct((TAPS * 24, HID), BF),
             jax.ShapeDtypeStruct((16, 2, HID), F32),
         ),
-        in_specs=[pl.BlockSpec(memory_space=pl.ANY)] * 4,
-        out_specs=(pl.BlockSpec(memory_space=pl.ANY),) * 4,
-        scratch_shapes=[pltpu.SemaphoreType.DMA((OWN + 4,))],
+        in_specs=[pl.BlockSpec(memory_space=vm)] * 4,
+        out_specs=(pl.BlockSpec(memory_space=vm),) * 4,
     )(*outs)
     return wg.transpose(0, 2, 1, 3), bg.T, hg.reshape(TAPS, 24, HID).transpose(1, 0, 2), fg
 

time: 139 us -> 129 us (0.928)
  the two profiles are of different devices: /device:TPU:1 before, /device:TPU:48 now
where the time goes in v7:
time: 129 us; the launch traced here: 128 us
  Pallas kernels  111 us (86%)
  local copies, waits for them, and re-layouts  15.6 us (12%)
  between operations  1.32 us (1%)
    pallas_call x1, Pallas kernels, shards(): pl.pallas_call(kernel, out_shape=(jax.ShapeDtypeStruct((OWN * TAPS * GATE...  109 us
    unnamed x34, local copies, waits for them, and re-layouts  15.6 us

profile of v7, /device:TPU:48, one launch (start us, length us, event | category | flops | bytes accessed | tf_op | source)
XLA Modules:
  0.0 128.0 jit_solution(15278256503038015170)
XLA Ops:
  1.3 0.0 copy-start
  1.3 1.7 %copy-done = bf16[384,9,384]{2,0,1:T(8,128)(2,1)S(1)} copy-done((bf16[384,9,384]{2,0,1:T(8,128)(2,1)S(1)}, bf16[384,9,384]{2,0,1:T(8,128)(2,1)}, u32[]{:S(2)}) %copy-start) | copy-done | bytes 2654232
  3.0 0.0 copy-start.1
  3.0 1.1 copy-done.1
  4.1 0.0 copy-start.3
  4.1 1.0 copy-done.3
  5.1 0.0 copy-start.4
  5.1 1.0 copy-done.4
  6.1 0.0 copy-start.5
  6.1 1.0 copy-done.5
  7.2 0.0 copy-start.6
  7.2 1.0 copy-done.6
  8.2 0.0 copy-start.7
  8.2 1.0 copy-done.7
  9.2 0.0 copy-start.8
  9.2 1.0 copy-done.8
  10.2 0.0 copy-start.9
  10.2 1.0 copy-done.9
  11.1 0.0 copy-start.11
  11.1 0.9 copy-done.11
  12.0 0.0 copy-start.12
  12.0 0.8 copy-done.12
  12.8 0.0 copy-start.14
  12.8 0.7 copy-done.14
  13.5 0.0 copy-start.15
  13.5 0.7 copy-done.15
  14.2 108.9 %shard_map.165 = (bf16[432,768]{1,0:T(8,128)(2,1)S(1)}, f32[4,12]{1,0:T(4,128)S(1)}, bf16[216,384]{1,0:T(8,128)(2,1)S(1)}, f32[16,2,384]{2,1,0:T(2,128)S(1)}) custom-call(bf16[12,9,4,768]{3,2,1,0:T(4,128)(2,1)S(1)} %bitcast.13, bf16[432,432]{1,0:T(8,128)(2,1)S(1)} %copy-done.5, bf16[3,384,128]{2,1,0:T(8,128)(2,1)S(1)} %bitcast.14, f32[4,12]{1,0:T(4,128)S(1)} %bitcast.16, ...), custom_call_target="tpu_custom_call" | custom-call | tf_op jit(solution)/shard_map/pallas_call | solution.py:652
  123.1 0.0 copy-start.2
  123.1 0.8 copy-done.2
  124.0 0.0 copy-start.10
  124.0 0.7 copy-done.10
  124.7 0.0 copy-start.13
  124.7 0.6 copy-done.13
  125.3 0.0 copy-start.16
  125.3 0.6 copy-done.16
  125.8 2.2 %shard_map.166 = (bf16[12,9,4,768]{3,2,1,0:T(4,128)(2,1)}, f32[4,12]{1,0:T(4,128)}, bf16[216,384]{1,0:T(8,128)(2,1)}, f32[16,2,384]{2,1,0:T(2,128)}) custom-call(bf16[432,768]{1,0:T(8,128)(2,1)} %copy-done.2, f32[4,12]{1,0:T(4,128)} %copy-done.16, bf16[216,384]{1,0:T(8,128)(2,1)} %copy-done.10, f32[16,2,384]{2,1,0:T(2,128)} %copy-done.13), custom_call_target="tpu_custom_call" | custom-call | tf_op jit(solution)/shard_map/pallas_call | solution.py:717
Async XLA Ops:
  1.3 1.8 %copy-start = (bf16[384,9,384]{2,0,1:T(8,128)(2,1)S(1)}, bf16[384,9,384]{2,0,1:T(8,128)(2,1)}, u32[]{:S(2)}) copy-start(bf16[384,9,384]{2,0,1:T(8,128)(2,1)} %param.17) | copy-start | bytes 7962628
  3.0 1.1 copy-start.1
  4.1 1.0 copy-start.3
  5.1 1.0 copy-start.4
  6.1 1.0 copy-start.5
  7.2 1.0 copy-start.6
  8.2 1.0 copy-start.7
  9.2 1.0 copy-start.8
  10.2 1.0 copy-start.9
  11.1 0.9 copy-start.11
  12.0 0.8 copy-start.12
  12.8 0.7 copy-start.14
  13.5 0.7 copy-start.15
  123.1 0.9 copy-start.2
  124.0 0.7 copy-start.10
  124.7 0.6 copy-start.13
  125.3 0.6 copy-start.16

commit v8 on v7

--- a/solution.py
+++ b/solution.py
@@ -711,7 +711,7 @@
             pltpu.SemaphoreType.DMA((N_IN - 1,)),
         ],
         compiler_params=pltpu.CompilerParams(
-            collective_id=0, has_side_effects=True, vmem_limit_bytes=24 * 2**20
+            collective_id=0, has_side_effects=True, vmem_limit_bytes=56 * 2**20
         ),
     )(*inputs, lead_index)
     wg, bg, hg, fg = pl.pallas_call(

time: 129 us -> 113 us (0.88)
  the two profiles are of different devices: /device:TPU:48 before, /device:TPU:1 now
where the time goes in v8:
time: 113 us; the launch traced here: 112 us
  Pallas kernels  111 us (98%)
  between operations  1.29 us (1%)
    pallas_call x1, Pallas kernels, shards(): pl.pallas_call(kernel, out_shape=(jax.ShapeDtypeStruct((OWN * TAPS * GATE...  108 us

profile of v8, /device:TPU:1, one launch (start us, length us, event | category | flops | bytes accessed | tf_op | source)
XLA Modules:
  0.0 111.8 jit_solution(5569477409983448592)
XLA Ops:
  1.3 108.3 %shard_map.165 = (bf16[432,768]{1,0:T(8,128)(2,1)}, f32[4,12]{1,0:T(4,128)}, bf16[216,384]{1,0:T(8,128)(2,1)}, f32[16,2,384]{2,1,0:T(2,128)}) custom-call(bf16[12,9,4,768]{3,2,1,0:T(4,128)(2,1)} %bitcast.13, bf16[432,432]{1,0:T(8,128)(2,1)} %constant.14.clone.refs_1_, bf16[3,384,128]{2,1,0:T(8,128)(2,1)} %bitcast.14, f32[4,12]{1,0:T(4,128)} %bitcast.16, ...), custom_call_target="tpu_custom_call" | custom-call | tf_op jit(solution)/shard_map/pallas_call | solution.py:652
  109.6 2.2 %shard_map.166 = (bf16[12,9,4,768]{3,2,1,0:T(4,128)(2,1)}, f32[4,12]{1,0:T(4,128)}, bf16[216,384]{1,0:T(8,128)(2,1)}, f32[16,2,384]{2,1,0:T(2,128)}) custom-call(bf16[432,768]{1,0:T(8,128)(2,1)} %get-tuple-element.12.wg, f32[4,12]{1,0:T(4,128)} %get-tuple-element.13.bg, bf16[216,384]{1,0:T(8,128)(2,1)} %get-tuple-element.14.hg, ...), custom_call_target="tpu_custom_call" | custom-call | tf_op jit(solution)/shard_map/pallas_call | solution.py:717

commit v9 on v8

--- a/solution.py
+++ b/solution.py
@@ -414,7 +414,7 @@
                 scat[2 * PAD:4 * PAD, pl.ds(at, W)] = hblk[t - 1, r].reshape(2 * PAD, W)
             return carry
 
-        lax.fori_loop(0, T, body, 0, unroll=8)
+        lax.fori_loop(0, T, body, 0, unroll=16)
         return jnp.concatenate([nt(stack[:, (2 - a) * W:(2 - a + T) * W], scat[...]) for a in range(3)], 0).T
 
     def share_weights(n, x):
@@ -489,7 +489,7 @@
         vv[0:96, pl.ds(pl.multiple_of(r * W, W), W)] = (uq * jax.nn.sigmoid(uq)).astype(BF)
         return carry
 
-    lax.fori_loop(0, T, head_rows, 0)
+    lax.fori_loop(0, T, head_rows, 0, unroll=4)
     for a in range(3):
         first = (4 - 2 * a) * W
         part = nt(cc[:, first:first + T * W], vv[...])

time: 113 us -> 112 us (level)
  the two profiles are of different devices: /device:TPU:1 before, /device:TPU:8 now
where the time goes in v9:
time: 112 us
  Pallas kernels  111 us (99%)
  between operations  1.29 us (1%)
    pallas_call x1, Pallas kernels, shards(): pl.pallas_call(kernel, out_shape=(jax.ShapeDtypeStruct((OWN * TAPS * GATE...  109 us

profile of v9, /device:TPU:8, one launch (start us, length us, event | category | flops | bytes accessed | tf_op | source)
XLA Modules:
  0.0 112.2 jit_solution(6939085639443415606)
XLA Ops:
  1.3 108.7 %shard_map.165 = (bf16[432,768]{1,0:T(8,128)(2,1)}, f32[4,12]{1,0:T(4,128)}, bf16[216,384]{1,0:T(8,128)(2,1)}, f32[16,2,384]{2,1,0:T(2,128)}) custom-call(bf16[12,9,4,768]{3,2,1,0:T(4,128)(2,1)} %bitcast.13, bf16[432,432]{1,0:T(8,128)(2,1)} %constant.14.clone.refs_1_, bf16[3,384,128]{2,1,0:T(8,128)(2,1)} %bitcast.14, f32[4,12]{1,0:T(4,128)} %bitcast.16, ...), custom_call_target="tpu_custom_call" | custom-call | tf_op jit(solution)/shard_map/pallas_call | solution.py:652
  110.0 2.2 %shard_map.166 = (bf16[12,9,4,768]{3,2,1,0:T(4,128)(2,1)}, f32[4,12]{1,0:T(4,128)}, bf16[216,384]{1,0:T(8,128)(2,1)}, f32[16,2,384]{2,1,0:T(2,128)}) custom-call(bf16[432,768]{1,0:T(8,128)(2,1)} %get-tuple-element.12.wg, f32[4,12]{1,0:T(4,128)} %get-tuple-element.13.bg, bf16[216,384]{1,0:T(8,128)(2,1)} %get-tuple-element.14.hg, ...), custom_call_target="tpu_custom_call" | custom-call | tf_op jit(solution)/shard_map/pallas_call | solution.py:717
